TPU v7x, 256 devices: a whole 4x4x8 slice. The times are simulated.
256 devices in a mesh: tok: 64 (over z, y, core), tp: 4 (over x).
Axes of the slice: x: 4, y: 4, z: 8, core: 2. Of those that a mesh axis runs over, the one named last changes fastest.
Arguments:
- attended: bfloat16 [32768, 4096], P('tok', 'tp'), may hold values from -6 to 6
- token_adapter: int32 [32768, 1], P('tok'), may hold values from 0 to 127; in each aligned block of 512 rows (0 to 511, 512 to 1023, ...) at most 6 rows name the same one
- adapter_slot: int32 [128], replicated, may hold values from 0 to 127, each once
- output_weight: bfloat16 [4096, 4096], P('tp'), may hold values from -0.09375 to 0.09375
- adapter_down: bfloat16 [128, 64, 4096], P('tok', None, 'tp'), may hold values from -0.09375 to 0.09375
- adapter_up: bfloat16 [128, 64, 4096], P('tok'), may hold values from -0.75 to 0.75
- block_values: bfloat16 [128, 32, 2, 128, 128], P('tok', 'tp'), may hold values from -0.375 to 0.375
- block_columns: int32 [128, 32, 2], P('tok', 'tp'), may hold values from 0 to 31
Outputs:
- projected: bfloat16 [32768, 4096], P('tok', 'tp')
Inputs may be any that keep to these rules, and one draw needn't show every extreme that they name: `token_adapter`: among the 512 tokens of one index of tok, at most 6 name the same adapter; in every draw some adapter is named by exactly 6 tokens of some index of tok. `adapter_slot`: every slot is taken by exactly one adapter.
All inputs are finite; a program needn't handle non-finite values.
Results may differ from a plain program's by a relative error of at most 0.015.
Values may be sent and summed in bfloat16 or wider, within the bound.
No kernel may reach another device: no remote copies, remote signals or barrier semaphores. Data moves between devices by JAX's collectives and lax.ppermute only.
A program may use at most 128 MiB of HBM per device.

v0:
```python
import jax
import jax.numpy as jnp
from jax import lax
from jax.sharding import PartitionSpec as P

BLOCK = 128


adapter_delta_scale = 2.0


def on_device(
    attended,
    token_adapter,
    adapter_slot,
    output_weight,
    adapter_down,
    adapter_up,
    block_values,
    block_columns,
):
    tok_dev, width_part = attended.shape
    adapters = adapter_slot.shape[0]
    owner_tokens = lax.axis_size("tok")
    device_slots = adapter_down.shape[0]
    token_capacity = max(2, 3 * tok_dev // (2 * adapters))
    projection_width = adapter_up.shape[2]
    row_blocks = block_values.shape[1]
    per_row = block_values.shape[2]
    column_blocks = projection_width // BLOCK
    catalog = jnp.arange(adapters, dtype=jnp.int32)
    adapter_of = token_adapter[:, 0]
    token_slot = jnp.sum(
        jnp.where(adapter_of[:, None] == catalog[None, :], adapter_slot[None, :], 0), axis=1
    )
    member = (token_slot[:, None] == catalog[None, :]).astype(jnp.int32)
    position = jnp.sum(member * jnp.cumsum(member, axis=0), axis=1) - 1
    target = token_slot * token_capacity + position
    outgoing = (
        jnp.zeros((adapters * token_capacity, width_part), attended.dtype).at[target].set(attended)
    )
    incoming = lax.all_to_all(outgoing, "tok", split_axis=0, concat_axis=0, tiled=True)
    incoming = incoming.reshape(owner_tokens, device_slots, token_capacity, width_part)
    base_part = jnp.dot(attended, output_weight, preferred_element_type=jnp.float32)
    shrunk = jnp.einsum(
        "jscd,srd->jscr", incoming, adapter_down, preferred_element_type=jnp.float32
    ).astype(jnp.bfloat16)
    rank_factors = jnp.einsum(
        "jscr,sre->jsce", shrunk, adapter_up, preferred_element_type=jnp.float32
    )
    pieces = incoming.reshape(owner_tokens, device_slots, token_capacity, row_blocks, BLOCK)
    block_out = jnp.einsum(
        "jscrk,srbkm->jscrbm", pieces, block_values, preferred_element_type=jnp.float32
    )
    placement = (
        block_columns.reshape(device_slots, row_blocks * per_row, 1)
        == jnp.arange(column_blocks, dtype=jnp.int32)[None, None, :]
    ).astype(jnp.float32)
    sparse_blocks = jnp.einsum(
        "jscqm,sqe->jscem",
        block_out.reshape(owner_tokens, device_slots, token_capacity, row_blocks * per_row, BLOCK),
        placement,
        precision=lax.Precision.HIGHEST,
    )
    deltas = (
        adapter_delta_scale * rank_factors
        + sparse_blocks.reshape(owner_tokens, device_slots, token_capacity, projection_width)
    ).astype(jnp.bfloat16)
    returned = lax.all_to_all(
        deltas.reshape(adapters * token_capacity, projection_width),
        "tok",
        split_axis=0,
        concat_axis=0,
        tiled=True,
    )
    own_rows = jnp.take(returned, target, axis=0).astype(jnp.float32)
    summed = lax.psum_scatter(
        (base_part + own_rows).astype(jnp.bfloat16), "tp", scatter_dimension=1, tiled=True
    )
    return summed


def solution(mesh):
    placed = (
        P("tok", "tp"),
        P("tok", None),
        P(),
        P("tp", None),
        P("tok", None, "tp"),
        P("tok", None, None),
        P("tok", "tp", None, None, None),
        P("tok", "tp", None),
    )
    return jax.shard_map(
        on_device, mesh=mesh, in_specs=placed, out_specs=P("tok", "tp"), check_vma=False
    )
```

profile of v0, /device:TPU:1, one launch (start us, length us, event | category | flops | bytes accessed | tf_op | source)
XLA Modules:
  0.0 415.7 jit_solution(11950506224669403506)
XLA Ops:
  6.5 0.0 copy-start
  6.5 1.0 select_reduce_fusion
  7.6 0.1 copy.12
  7.7 0.2 fusion.15
  8.0 0.2 fusion.14
  8.3 3.7 scatter_custom_fusion
  12.0 1.5 all_to_all.14
  13.5 13.2 %all-to-all-start = ((bf16[64,12,1024]{2,1,0:T(8,128)(2,1)}), bf16[64,12,1024]{2,1,0:T(8,128)(2,1)S(1)}, u32[]{:S(2)}, u32[]{:S(2)}) async-start(bf16[64,12,1024]{2,1,0:T(8,128)(2,1)} %all_to_all.14), calls=%async_computation | async-start | bytes 4194304 | tf_op jit(solution)/shard_map/all_to_all | solution.py:42
  26.7 0.0 copy-done.3
  26.7 0.1 copy.15
  26.8 0.1 eq.64
  26.9 49.5 %all-to-all-done = bf16[64,12,1024]{2,1,0:T(8,128)(2,1)S(1)} async-done(((bf16[64,12,1024]{2,1,0:T(8,128)(2,1)}), bf16[64,12,1024]{2,1,0:T(8,128)(2,1)S(1)}, u32[]{:S(2)}, u32[]{:S(2)}) %all-to-all-start) | async-done | bytes 1572896 | tf_op jit(solution)/shard_map/all_to_all | solution.py:42
  76.3 2.0 reshape.98
  78.3 2.7 convolution_bitcast_fusion
  81.0 1.1 copy.18
  82.1 9.5 %fusion.3 = f32[64,2,6,32,128]{4,3,2,0,1:T(8,128)} fusion(f32[64,2,6,16,128]{4,0,3,2,1:T(8,128)S(1)} %bitcast.60, s32[2,16]{1,0:T(2,128)S(1)} %eq.64), kind=kOutput, calls=%fused_computation.7 | convolution fusion | flops 603980800 | bytes 18874496 | tf_op jit(solution)/shard_map/jscqm,sqe->jscem/dot_general | solution.py:59
  91.6 11.3 %copy.20 = f32[64,2,6,32,128]{4,3,0,2,1:T(8,128)} copy(f32[64,2,6,32,128]{4,3,2,0,1:T(8,128)} %fusion.3) | data formatting | bytes 25165824 | tf_op jit(solution)/shard_map/jscqm,sqe->jscem/transpose | solution.py:59
  102.9 13.8 %reshape.76 = f32[64,2,6,4096]{3,0,2,1:T(8,128)} reshape(f32[64,2,6,32,128]{4,3,0,2,1:T(8,128)} %copy.20) | data formatting | bytes 25165824 | tf_op jit(solution)/shard_map/reshape | solution.py:67
  116.7 2.1 copy.14
  118.8 0.0 copy-done
  118.8 0.0 copy-done.2
  118.8 8.1 %fusion = bf16[64,2,6,4096]{3,0,2,1:T(8,128)(2,1)} fusion(f32[64,2,6,4096]{3,0,2,1:T(8,128)} %reshape.76, bf16[64,2,6,1024]{3,0,2,1:T(8,128)(2,1)} %bitcast.63, bf16[2,64,4096]{2,1,0:T(8,128)(2,1)S(1)} %copy-done, bf16[2,64,1024]{2,1,0:T(8,128)(2,1)S(1)} %copy-done.2), kind=kOutput, calls=%fused_computation.3 | convolution fusion | flops 512802816 | bytes 21757952 | tf_op jit(solution)/shard_map/jscr,sre->jsce/dot_general | solution.py:48
  126.9 9.6 %copy.21 = bf16[64,12,4096]{2,1,0:T(8,128)(2,1)} copy(bf16[64,12,4096]{2,0,1:T(8,128)(2,1)} %bitcast.61) | data formatting | bytes 12582912 | tf_op jit(solution)/shard_map/all_to_all | solution.py:69
  136.5 7.2 %all-to-all-start.1 = ((bf16[64,12,4096]{2,1,0:T(8,128)(2,1)}), bf16[64,12,4096]{2,1,0:T(8,128)(2,1)}, u32[]{:S(2)}, u32[]{:S(2)}) async-start(bf16[64,12,4096]{2,1,0:T(8,128)(2,1)} %copy.21), calls=%async_computation.1 | async-start | bytes 16777216 | tf_op jit(solution)/shard_map/all_to_all | solution.py:69
  143.8 0.0 reduce-scatter.2.cloned.1.call-start
  143.8 182.8 %all-to-all-done.1 = bf16[64,12,4096]{2,1,0:T(8,128)(2,1)} async-done(((bf16[64,12,4096]{2,1,0:T(8,128)(2,1)}), bf16[64,12,4096]{2,1,0:T(8,128)(2,1)}, u32[]{:S(2)}, u32[]{:S(2)}) %all-to-all-start.1) | async-done | bytes 6291488 | tf_op jit(solution)/shard_map/all_to_all | solution.py:69
  326.7 9.9 %all_to_all.18 = bf16[768,4096]{1,0:T(8,128)(2,1)} reshape(bf16[64,12,4096]{2,1,0:T(8,128)(2,1)} %all-to-all-done.1) | data formatting | bytes 12582912 | tf_op jit(solution)/shard_map/all_to_all | solution.py:69
  336.5 12.2 %gather_fusion = bf16[512,4096]{1,0:T(8,128)(2,1)} fusion(bf16[768,4096]{1,0:T(8,128)(2,1)} %all_to_all.18, s32[1024]{0:T(1024)S(1)} %pad_clamp_fusion), kind=kCustom, calls=%fused_computation | custom fusion | bytes 8390656 | tf_op jit(solution)/shard_map/jit(_take)/gather | solution.py:76
  348.8 0.0 copy-done.4
  348.8 10.2 %add_convert_fusion = bf16[512,4096]{1,0:T(8,128)(2,1)} fusion(bf16[512,1024]{1,0:T(8,128)(2,1)S(1)} %copy-done.4, bf16[1024,4096]{1,0:T(8,128)(2,1)} %param.11, bf16[512,4096]{1,0:T(8,128)(2,1)} %gather_fusion, pred[512]{0:T(512)(128)(4,1)S(1)} %get-tuple-element.5), kind=kOutput, calls=%fused_computation.4 | convolution fusion | flops 4303355904 | bytes 17826304 | tf_op jit(solution)/shard_map/dot_general | solution.py:44
  359.0 0.0 reduce-scatter.2.cloned.1.call-update
  359.0 49.9 %reduce-scatter.2.cloned.1.call-done = bf16[512,1024]{1,0:T(8,128)(2,1)} async-done(((bf16[512,4096]{1,0:T(8,128)(2,1)}), bf16[512,1024]{1,0:T(8,128)(2,1)}) %reduce-scatter.2.cloned.1.call-update) | async-done | bytes 1048592 | tf_op jit(solution)/shard_map/reduce_scatter | solution.py:77
  (14 shorter events, 0.1 us)
Async XLA Ops:
  6.5 112.3 %copy-start = (bf16[2,64,4096]{2,1,0:T(8,128)(2,1)S(1)}, bf16[2,64,4096]{2,1,0:T(8,128)(2,1)}, u32[]{:S(2)}) copy-start(bf16[2,64,4096]{2,1,0:T(8,128)(2,1)} %param.13) | copy-start | bytes 3145732
  6.5 20.1 %copy-start.3 = (s32[2,8,2]{1,2,0:T(2,128)S(1)}, s32[2,8,2]{1,2,0:T(2,128)}, u32[]{:S(2)}) copy-start(s32[2,8,2]{1,2,0:T(2,128)} %param.15) | copy-start | bytes 388
  13.5 62.8 %all-to-all-start = ((bf16[64,12,1024]{2,1,0:T(8,128)(2,1)}), bf16[64,12,1024]{2,1,0:T(8,128)(2,1)S(1)}, u32[]{:S(2)}, u32[]{:S(2)}) async-start(bf16[64,12,1024]{2,1,0:T(8,128)(2,1)} %all_to_all.14), calls=%async_computation | async-start | bytes 4194304 | tf_op jit(solution)/shard_map/all_to_all | solution.py:42
  102.9 15.9 %copy-start.2 = (bf16[2,64,1024]{2,1,0:T(8,128)(2,1)S(1)}, bf16[2,64,1024]{2,1,0:T(8,128)(2,1)}, u32[]{:S(2)}) copy-start(bf16[2,64,1024]{2,1,0:T(8,128)(2,1)} %param.12) | copy-start | bytes 786436
  136.5 190.1 %all-to-all-start.1 = ((bf16[64,12,4096]{2,1,0:T(8,128)(2,1)}), bf16[64,12,4096]{2,1,0:T(8,128)(2,1)}, u32[]{:S(2)}, u32[]{:S(2)}) async-start(bf16[64,12,4096]{2,1,0:T(8,128)(2,1)} %copy.21), calls=%async_computation.1 | async-start | bytes 16777216 | tf_op jit(solution)/shard_map/all_to_all | solution.py:69
  143.8 265.1 %reduce-scatter.2.cloned.1.call-start = ((), (), s32[]{:S(2)}) async-start(), calls=%async_computation.3 | async-start | bytes 5242880 | tf_op jit(solution)/shard_map/reduce_scatter | solution.py:77
  336.5 12.2 %copy-start.4 = (bf16[512,1024]{1,0:T(8,128)(2,1)S(1)}, bf16[512,1024]{1,0:T(8,128)(2,1)}, u32[]{:S(2)}) copy-start(bf16[512,1024]{1,0:T(8,128)(2,1)} %param.8) | copy-start | bytes 3145732
  348.8 60.1 %copy-start.1 = (bf16[2,64,4096]{2,1,0:T(8,128)(2,1)S(1)}, bf16[2,64,4096]{2,1,0:T(8,128)(2,1)}, u32[]{:S(2)}) copy-start(bf16[2,64,4096]{2,1,0:T(8,128)(2,1)} %param.13) | copy-start | bytes 3145732
Sparse Core Ops, SparseCore 0:
  359.1 49.7 reduce-scatter.1
where the time goes:
time: 417 us; the launch traced here: 416 us
  waiting for transfers between devices  282 us (68%)
  local copies, waits for them, and re-layouts  67.6 us (16%)
  matrix products  30.5 us (7%)
  starting transfers between devices  20.5 us (5%)
  between operations  13.5 us (3%)
    all_to_all x1, waiting for transfers between devices, on_device(): lax.all_to_all(deltas.reshape(adapters * token_capacity, projection_width...  183 us
    reduce_scatter x1, waiting for transfers between devices, on_device(): lax.psum_scatter((base_part + own_rows).astype(jnp.bfloat16), 'tp', scatt...  49.9 us
    all_to_all x1, waiting for transfers between devices, on_device(): lax.all_to_all(outgoing, 'tok', split_axis=0, concat_axis=0, tiled=True)  49.5 us
    all_to_all x2, local copies, waits for them, and re-layouts, on_device(): lax.all_to_all(deltas.reshape(adapters * token_capacity, projection_width...  19.4 us
    reshape x1, local copies, waits for them, and re-layouts, on_device(): sparse_blocks.reshape(owner_tokens, device_slots, token_capacity, project...  13.8 us
    all_to_all x1, starting transfers between devices, on_device(): lax.all_to_all(outgoing, 'tok', split_axis=0, concat_axis=0, tiled=True)  13.2 us
    gather x1, local copies, waits for them, and re-layouts, on_device(): own_rows = jnp.take(returned, target, axis=0).astype(jnp.float32)  12.2 us
    transpose x1, local copies, waits for them, and re-layouts, on_device(): jnp.einsum('jscqm,sqe->jscem', block_out.reshape(owner_tokens, device_slo...  11.3 us
  transfers between devices with their start and end apart: 3, of which 3 were waited for; matrix products, arithmetic and copies ran while one was open for 0% of the time, Pallas kernels for 0%

commit v1 on v0

v1 whole, which is shorter than its diff:
```python
import functools

import jax
import jax.numpy as jnp
from jax import lax
from jax.experimental import pallas as pl
from jax.experimental.pallas import tpu as pltpu
from jax.sharding import PartitionSpec as P

BLOCK = 128
CAP = 6
SCALE = 2.0
VMEM = pl.BlockSpec(memory_space=pltpu.VMEM)
SMEM = pl.BlockSpec(memory_space=pltpu.SMEM)
PARAMS = pltpu.CompilerParams(vmem_limit_bytes=40 * 1024 * 1024)
f32, bf16, i32 = jnp.float32, jnp.bfloat16, jnp.int32


def iota(shape, dim):
    return lax.broadcasted_iota(i32, shape, dim)


def dot(a, b, dims=((1,), (0,))):
    return lax.dot_general(a, b, (dims, ((), ())), preferred_element_type=f32)


def pack_kernel(n_tok, n_tp, adapter_ref, slot_ref, x_ref, out_ref, target_ref, wide):
    tokens, width = x_ref.shape
    slots = slot_ref.shape[1]
    pieces = width // BLOCK
    half = CAP // 2
    own_slots = slots // n_tok
    named = (iota((slots, tokens), 0) == adapter_ref[...]).astype(bf16)
    held = (iota((slots, slots), 0) == slot_ref[...]).astype(bf16)
    member = dot(held, named)
    before = (iota((tokens, tokens), 0) < iota((tokens, tokens), 1)).astype(bf16)
    count = dot(member.astype(bf16), before)
    rank = jnp.sum(member * count, axis=0, keepdims=True)
    slot = iota((slots, tokens), 0)
    base = (slot % own_slots) * (2 * n_tok * half) + (slot // own_slots) * half
    start = jnp.sum(member * base.astype(f32), axis=0, keepdims=True)
    place = jnp.where(rank >= half, rank + (n_tok * half - half), rank)
    target = (start + place).astype(i32)
    eye = iota((tokens, tokens), 0) == iota((tokens, tokens), 1)
    target_ref[...] = jnp.sum(jnp.where(eye, target, 0), axis=1, keepdims=True)
    rows = slots * CAP
    pick = (iota((rows, tokens), 0) == target).astype(bf16)
    for j in range(0, pieces, 2):
        both = dot(pick, x_ref[:, j * BLOCK : (j + 2) * BLOCK])
        wide[pl.ds(j, rows, stride=pieces), :] = both[:, :BLOCK]
        wide[pl.ds(j + 1, rows, stride=pieces), :] = both[:, BLOCK:]
    out_ref[...] = wide[...].astype(bf16)


def delta_kernel(groups, meta_ref, x_ref, w_ref, up_ref, out_ref, wide, terms, sums):
    all_rows = x_ref.shape[0]
    rank = up_ref.shape[1]
    columns = up_ref.shape[2] // BLOCK
    per_group = all_rows // groups
    pieces = columns // groups
    rows = per_group // pieces
    slot = meta_ref[0]
    wide[...] = x_ref[...].astype(f32)
    shrunk = jnp.zeros((rows, rank), f32)
    down_at = pieces * 2 * BLOCK
    for g in range(groups):
        for j in range(pieces):
            r = g * pieces + j
            x = wide[pl.ds(g * per_group + j, rows, stride=pieces), :].astype(bf16)
            terms[2 * r] = dot(x, w_ref[g, (2 * j) * BLOCK : (2 * j + 1) * BLOCK, :])
            terms[2 * r + 1] = dot(x, w_ref[g, (2 * j + 1) * BLOCK : (2 * j + 2) * BLOCK, :])
            down = w_ref[g, down_at + j * rank : down_at + (j + 1) * rank, :]
            shrunk = shrunk + dot(x, down, ((1,), (1,)))
    small = (SCALE * shrunk).astype(bf16)
    up = up_ref[slot]
    for c in range(0, columns, 2):
        both = dot(small, up[:, c * BLOCK : (c + 2) * BLOCK])
        sums[c] = both[:, :BLOCK]
        sums[c + 1] = both[:, BLOCK:]
    for q in range(2 * columns):
        c = meta_ref[1 + q]
        sums[c] = sums[c] + terms[q]
    for c in range(columns):
        g, j = divmod(c, pieces)
        wide[pl.ds(g * per_group + j, rows, stride=pieces), :] = sums[c]
    out_ref[...] = wide[...].astype(bf16)


def finish_kernel(target_ref, back_ref, base_ref, out_ref, wide):
    tokens, width = base_ref.shape
    pieces = width // BLOCK
    rows = back_ref.shape[0] // pieces
    wide[...] = back_ref[...].astype(f32)
    pick = (iota((tokens, rows), 1) == target_ref[...]).astype(bf16)
    for j in range(pieces):
        part = wide[pl.ds(j, rows, stride=pieces), :].astype(bf16)
        at = slice(j * BLOCK, (j + 1) * BLOCK)
        out_ref[:, at] = (dot(pick, part) + base_ref[:, at].astype(f32)).astype(bf16)


def cost(flops, moved):
    return pl.CostEstimate(flops=flops, bytes_accessed=moved, transcendentals=0)


def on_device(
    attended,
    token_adapter,
    adapter_slot,
    output_weight,
    adapter_down,
    adapter_up,
    block_values,
    block_columns,
):
    tokens, width = attended.shape
    slots = adapter_slot.shape[0]
    n_tok, n_tp = lax.axis_size("tok"), lax.axis_size("tp")
    own, rank = adapter_down.shape[:2]
    columns = adapter_up.shape[2]
    pieces = width // BLOCK
    lines = slots * CAP * pieces
    share = n_tp // own

    down = jnp.swapaxes(adapter_down.reshape(own, rank, pieces, BLOCK), 1, 2)
    weights = jnp.concatenate(
        [
            block_values.reshape(own, pieces * 2 * BLOCK, BLOCK),
            down.reshape(own, pieces * rank, BLOCK),
        ],
        axis=1,
    )
    weights = jnp.repeat(weights, share, axis=0)
    weights = lax.all_to_all(weights, "tp", 0, 0, tiled=True)
    places = jnp.repeat(block_columns.reshape(own, pieces * 2), share, axis=0)
    places = lax.all_to_all(places, "tp", 0, 0, tiled=True)
    mine = (lax.axis_index("tp") // share).astype(i32)
    meta = jnp.concatenate([mine[None], places.reshape(-1)])

    packed, target = pl.pallas_call(
        functools.partial(pack_kernel, n_tok, n_tp),
        out_shape=(
            jax.ShapeDtypeStruct((lines, BLOCK), bf16),
            jax.ShapeDtypeStruct((tokens, 1), i32),
        ),
        in_specs=[VMEM, VMEM, VMEM],
        out_specs=(VMEM, VMEM),
        scratch_shapes=[pltpu.VMEM((lines, BLOCK), f32)],
        compiler_params=PARAMS,
        cost_estimate=cost(2 * lines // pieces * tokens * width, 6 * lines * BLOCK),
        name="pack_rows",
    )(token_adapter.reshape(1, tokens), adapter_slot.reshape(1, slots), attended)
    came = lax.all_to_all(packed, ("tp", "tok"), 0, 0, tiled=True)

    base = jnp.dot(attended, output_weight, preferred_element_type=f32).astype(bf16)
    base = lax.psum_scatter(base, "tp", scatter_dimension=1, tiled=True)

    rows = lines // pieces // n_tp
    deltas = pl.pallas_call(
        functools.partial(delta_kernel, n_tp),
        out_shape=jax.ShapeDtypeStruct((lines, BLOCK), bf16),
        in_specs=[SMEM, VMEM, VMEM, VMEM],
        out_specs=VMEM,
        scratch_shapes=[
            pltpu.VMEM((lines, BLOCK), f32),
            pltpu.VMEM((2 * columns // BLOCK, rows, BLOCK), f32),
            pltpu.VMEM((columns // BLOCK, rows, BLOCK), f32),
        ],
        compiler_params=PARAMS,
        cost_estimate=cost(6 * rows * columns * 2 * BLOCK, 8 * lines * BLOCK),
        name="slot_deltas",
    )(meta, came, weights, adapter_up)
    back = lax.all_to_all(deltas, ("tp", "tok"), 0, 0, tiled=True)

    return pl.pallas_call(
        finish_kernel,
        out_shape=jax.ShapeDtypeStruct((tokens, width), bf16),
        in_specs=[VMEM, VMEM, VMEM],
        out_specs=VMEM,
        scratch_shapes=[pltpu.VMEM((lines, BLOCK), f32)],
        compiler_params=PARAMS,
        cost_estimate=cost(2 * lines // pieces * tokens * width, 6 * lines * BLOCK),
        name="add_deltas",
    )(target, back, base)


def solution(mesh):
    placed = (
        P("tok", "tp"),
        P("tok", None),
        P(),
        P("tp", None),
        P("tok", None, "tp"),
        P("tok", None, None),
        P("tok", "tp", None, None, None),
        P("tok", "tp", None),
    )
    return jax.shard_map(
        on_device, mesh=mesh, in_specs=placed, out_specs=P("tok", "tp"), check_vma=False
    )
```

time: 417 us -> 210 us (0.50)
  waiting for transfers between devices: 282 us -> 84.5 us
  local copies, waits for them, and re-layouts: 67.6 us -> 10 us
  blocking collectives: 0 us -> 48.4 us
  matrix products: 30.5 us -> 10.2 us
  starting transfers between devices: 20.5 us -> 31.8 us
  Pallas kernels: 0 us -> 9.81 us
    all_to_all x2 -> x3, waiting for transfers between devices: 232 us -> 84.5 us  [the longest x1 44.4 us: on_device(): weights = lax.all_to_all(weights, 'tp', 0, 0, tiled=True)]
    reduce_scatter x1, waiting for transfers between devices: 49.9 us -> 0.01 us  [on_device(): base = lax.psum_scatter(base, 'tp', scatter_dimension=1, tiled=True)]
    all_to_all x0 -> x1, blocking collectives: none -> 48.4 us  [on_device(): back = lax.all_to_all(deltas, ('tp', 'tok'), 0, 0, tiled=True)]
    all_to_all x4 -> x1, local copies, waits for them, and re-layouts: 23.1 us -> 0.51 us  [on_device(): places = lax.all_to_all(places, 'tp', 0, 0, tiled=True)]
    dot_general x4 -> x1, matrix products: 30.5 us -> 10.2 us  [on_device(): jnp.dot(attended, output_weight, preferred_element_type=f32).astype(bf16)]
    reshape x1 -> x2, local copies, waits for them, and re-layouts: 13.8 us -> 0.17 us  [the longest x1 0.09 us: on_device(): meta = jnp.concatenate([mine[None], places.reshape(-1)])]
    transpose x2, local copies, waits for them, and re-layouts: 12.4 us -> 0.06 us  [on_device(): down = jnp.swapaxes(adapter_down.reshape(own, rank, pieces, BLOCK), 1, 2)]
    gather x1 -> x0, local copies, waits for them, and re-layouts: 12.2 us -> none  [on_device(): own_rows = jnp.take(returned, target, axis=0).astype(jnp.float32)]
  transfers between devices with their start and end apart: 3 -> 4, of which waited for: 3 -> 2; matrix products, arithmetic and copies ran while one was open for 0% -> 6% of each run, Pallas kernels for 0% -> 3%
where the time goes in v1:
time: 210 us; the launch traced here: 209 us
  waiting for transfers between devices  84.5 us (40%)
  blocking collectives  48.4 us (23%)
  starting transfers between devices  31.8 us (15%)
  between operations  13.5 us (6%)
  matrix products  10.2 us (5%)
  local copies, waits for them, and re-layouts  10 us (5%)
  Pallas kernels  9.81 us (5%)
    all_to_all x1, blocking collectives, on_device(): back = lax.all_to_all(deltas, ('tp', 'tok'), 0, 0, tiled=True)  48.4 us
    all_to_all x1, waiting for transfers between devices, on_device(): weights = lax.all_to_all(weights, 'tp', 0, 0, tiled=True)  44.4 us
    all_to_all x1, waiting for transfers between devices, on_device(): came = lax.all_to_all(packed, ('tp', 'tok'), 0, 0, tiled=True)  40.1 us
    all_to_all x1, starting transfers between devices, on_device(): came = lax.all_to_all(packed, ('tp', 'tok'), 0, 0, tiled=True)  22.6 us
    dot_general x1, matrix products, on_device(): jnp.dot(attended, output_weight, preferred_element_type=f32).astype(bf16)  10.2 us
    unnamed x18, local copies, waits for them, and re-layouts  6.81 us
    pallas_call x1, Pallas kernels, on_device(): pl.pallas_call(functools.partial(delta_kernel, n_tp), out_shape=jax.Shape...  5.19 us
    all_to_all x1, starting transfers between devices, on_device(): places = lax.all_to_all(places, 'tp', 0, 0, tiled=True)  4.84 us
  transfers between devices with their start and end apart: 4, of which 2 were waited for; matrix products, arithmetic and copies ran while one was open for 6% of the time, Pallas kernels for 3%

profile of v1, /device:TPU:1, one launch (start us, length us, event | category | flops | bytes accessed | tf_op | source)
XLA Modules:
  0.0 209.0 jit_solution(5589187732565108530)
XLA Ops:
  6.5 0.8 copy.13
  7.3 0.1 reshape.35
  7.4 0.6 broadcast_in_dim.10
  8.0 4.8 %all-to-all-start = ((s32[4,1,16]{2,1,0:T(1,128)}), s32[4,1,16]{2,1,0:T(1,128)S(1)}, u32[]{:S(2)}, u32[]{:S(2)}) async-start(s32[4,1,16]{2,1,0:T(1,128)} %bitcast.4), calls=%async_computation | async-start | bytes 4096 | tf_op jit(solution)/shard_map/all_to_all | solution.py:135
  12.8 0.0 reduce-scatter.2.cloned.1.call-start
  12.8 10.2 %convolution_convert_fusion = bf16[512,4096]{1,0:T(8,128)(2,1)} fusion(bf16[512,1024]{1,0:T(8,128)(2,1)} %x_ref.1, bf16[1024,4096]{1,0:T(8,128)(2,1)} %param.11), kind=kOutput, calls=%fused_computation | convolution fusion | flops 4297064448 | bytes 13631488 | tf_op jit(solution)/shard_map/dot_general | solution.py:154
  23.0 0.0 copy-start.7
  23.0 0.0 reduce-scatter.2.cloned.1.call-update
  23.0 0.9 copy-done.7
  24.1 0.2 copy-done.6
  24.3 0.1 pad_maximum_fusion
  24.4 0.0 all-to-all-done
  24.4 1.9 broadcast_in_dim.11
  26.3 4.4 %all-to-all-start.2 = ((bf16[4,2560,128]{2,1,0:T(8,128)(2,1)}), bf16[4,2560,128]{2,1,0:T(8,128)(2,1)S(1)}, u32[]{:S(2)}, u32[]{:S(2)}) async-start(bf16[4,2560,128]{2,1,0:T(8,128)(2,1)} %bitcast.28), calls=%async_computation.2 | async-start | bytes 5242880 | tf_op jit(solution)/shard_map/all_to_all | solution.py:133
  30.6 0.0 copy-done.4
  30.6 0.0 copy-done.5
  30.7 1.2 copy-done.3
  31.9 1.6 pack_rows.1
  33.5 0.0 copy-start
  33.5 1.2 copy-done
  34.7 44.4 %all-to-all-done.2.w_ref = bf16[4,2560,128]{2,1,0:T(8,128)(2,1)S(1)} async-done(((bf16[4,2560,128]{2,1,0:T(8,128)(2,1)}), bf16[4,2560,128]{2,1,0:T(8,128)(2,1)S(1)}, u32[]{:S(2)}, u32[]{:S(2)}) %all-to-all-start.2) | async-done | bytes 2621472 | tf_op jit(solution)/shard_map/all_to_all | solution.py:133
  79.1 22.6 %all-to-all-start.1 = ((bf16[256,24,128]{2,1,0:T(8,128)(2,1)}), bf16[256,24,128]{2,1,0:T(8,128)(2,1)}, u32[]{:S(2)}, u32[]{:S(2)}) async-start(bf16[256,24,128]{2,1,0:T(8,128)(2,1)} %bitcast.25), calls=%async_computation.1 | async-start | bytes 3145728 | tf_op jit(solution)/shard_map/all_to_all | solution.py:152
  101.7 0.5 broadcast.4
  102.2 0.7 reduce.3
  102.9 0.1 reshape.36
  103.0 0.1 pad_add_fusion.meta_ref
  103.0 40.1 %all-to-all-done.1 = bf16[256,24,128]{2,1,0:T(8,128)(2,1)} async-done(((bf16[256,24,128]{2,1,0:T(8,128)(2,1)}), bf16[256,24,128]{2,1,0:T(8,128)(2,1)}, u32[]{:S(2)}, u32[]{:S(2)}) %all-to-all-start.1) | async-done | bytes 1572896 | tf_op jit(solution)/shard_map/all_to_all | solution.py:152
  143.1 1.2 copy-done.1
  144.3 5.2 %slot_deltas.1 = bf16[6144,128]{1,0:T(8,128)(2,1)S(1)} custom-call(s32[65]{0:T(128)S(1)} %pad_add_fusion.meta_ref, bf16[6144,128]{1,0:T(8,128)(2,1)} %bitcast.6.x_ref, bf16[4,2560,128]{2,1,0:T(8,128)(2,1)S(1)} %all-to-all-done.2.w_ref, bf16[2,64,4096]{2,1,0:T(8,128)(2,1)S(1)} %copy-done.1), custom_call_target="tpu_custom_call" | custom-call | flops 1207959552 | bytes 6291456 | tf_op jit(solution)/shard_map/slot_deltas/pallas_call | solution.py:158
  149.5 48.4 %all_to_all.36 = bf16[256,24,128]{2,1,0:T(8,128)(2,1)S(1)} all-to-all(bf16[256,24,128]{2,1,0:T(8,128)(2,1)S(1)} %bitcast.24), channel_id=1, replica_groups=mesh['tok'=64,'tp'=4] {'tp','tok'}, dimensions={0} | all-to-all | bytes 3145728 | tf_op jit(solution)/shard_map/all_to_all | solution.py:172
  197.9 1.2 copy-done.2
  199.1 3.0 %add_deltas.1 = bf16[512,1024]{1,0:T(8,128)(2,1)} custom-call(s32[512,1]{1,0:T(8,128)S(1)} %get-tuple-element.7.target_ref, bf16[6144,128]{1,0:T(8,128)(2,1)S(1)} %bitcast.23, bf16[512,1024]{1,0:T(8,128)(2,1)S(1)} %copy-done.2), custom_call_target="tpu_custom_call" | custom-call | flops 805306368 | bytes 4718592 | tf_op jit(solution)/shard_map/add_deltas/pallas_call | solution.py:174
  (10 shorter events, 0.1 us)
Async XLA Ops:
  8.0 16.4 %all-to-all-start = ((s32[4,1,16]{2,1,0:T(1,128)}), s32[4,1,16]{2,1,0:T(1,128)S(1)}, u32[]{:S(2)}, u32[]{:S(2)}) async-start(s32[4,1,16]{2,1,0:T(1,128)} %bitcast.4), calls=%async_computation | async-start | bytes 4096 | tf_op jit(solution)/shard_map/all_to_all | solution.py:135
  12.8 185.1 %reduce-scatter.2.cloned.1.call-start = ((), (), s32[]{:S(2)}) async-start(), calls=%async_computation.5 | async-start | bytes 5242880 | tf_op jit(solution)/shard_map/reduce_scatter | solution.py:155
  23.0 0.9 copy-start.7
  23.0 1.3 copy-start.6
  26.3 4.4 %copy-start.4 = (s32[512,1]{0,1:T(1,128)S(1)}, s32[512,1]{0,1:T(1,128)}, u32[]{:S(2)}) copy-start(s32[512,1]{0,1:T(1,128)} %param.9) | copy-start | bytes 6148
  26.3 4.4 %copy-start.5 = (s32[128]{0:T(128)S(1)}, s32[128]{0:T(128)}, u32[]{:S(2)}) copy-start(s32[128]{0:T(128)} %param.10) | copy-start | bytes 1540
  26.3 52.8 %all-to-all-start.2 = ((bf16[4,2560,128]{2,1,0:T(8,128)(2,1)}), bf16[4,2560,128]{2,1,0:T(8,128)(2,1)S(1)}, u32[]{:S(2)}, u32[]{:S(2)}) async-start(bf16[4,2560,128]{2,1,0:T(8,128)(2,1)} %bitcast.28), calls=%async_computation.2 | async-start | bytes 5242880 | tf_op jit(solution)/shard_map/all_to_all | solution.py:133
  30.7 1.2 copy-start.3
  33.5 1.2 copy-start
  79.1 64.0 %all-to-all-start.1 = ((bf16[256,24,128]{2,1,0:T(8,128)(2,1)}), bf16[256,24,128]{2,1,0:T(8,128)(2,1)}, u32[]{:S(2)}, u32[]{:S(2)}) async-start(bf16[256,24,128]{2,1,0:T(8,128)(2,1)} %bitcast.25), calls=%async_computation.1 | async-start | bytes 3145728 | tf_op jit(solution)/shard_map/all_to_all | solution.py:152
  143.1 1.2 copy-start.1
  197.9 1.2 copy-start.2
Sparse Core Ops, SparseCore 0:
  23.1 74.7 reduce-scatter.1

commit v2 on v1

--- a/solution.py
+++ b/solution.py
@@ -52,24 +52,27 @@
     out_ref[...] = wide[...].astype(bf16)
 
 
-def delta_kernel(groups, meta_ref, x_ref, w_ref, up_ref, out_ref, wide, terms, sums):
+def delta_kernel(groups, at_ref, place_ref, x_ref, up_ref, *refs):
+    w_refs, (out_ref, wide, terms, sums) = refs[:groups], refs[groups:]
     all_rows = x_ref.shape[0]
     rank = up_ref.shape[1]
     columns = up_ref.shape[2] // BLOCK
     per_group = all_rows // groups
     pieces = columns // groups
     rows = per_group // pieces
-    slot = meta_ref[0]
+    here, slot = at_ref[0], at_ref[1]
     wide[...] = x_ref[...].astype(f32)
     shrunk = jnp.zeros((rows, rank), f32)
     down_at = pieces * 2 * BLOCK
-    for g in range(groups):
+    for d in range(groups):
+        w_ref = w_refs[d]
+        g = lax.rem(here + groups - d, groups)
         for j in range(pieces):
-            r = g * pieces + j
+            r = d * pieces + j
             x = wide[pl.ds(g * per_group + j, rows, stride=pieces), :].astype(bf16)
-            terms[2 * r] = dot(x, w_ref[g, (2 * j) * BLOCK : (2 * j + 1) * BLOCK, :])
-            terms[2 * r + 1] = dot(x, w_ref[g, (2 * j + 1) * BLOCK : (2 * j + 2) * BLOCK, :])
-            down = w_ref[g, down_at + j * rank : down_at + (j + 1) * rank, :]
+            terms[2 * r] = dot(x, w_ref[(2 * j) * BLOCK : (2 * j + 1) * BLOCK, :])
+            terms[2 * r + 1] = dot(x, w_ref[(2 * j + 1) * BLOCK : (2 * j + 2) * BLOCK, :])
+            down = w_ref[down_at + j * rank : down_at + (j + 1) * rank, :]
             shrunk = shrunk + dot(x, down, ((1,), (1,)))
     small = (SCALE * shrunk).astype(bf16)
     up = up_ref[slot]
@@ -77,9 +80,10 @@
         both = dot(small, up[:, c * BLOCK : (c + 2) * BLOCK])
         sums[c] = both[:, :BLOCK]
         sums[c + 1] = both[:, BLOCK:]
-    for q in range(2 * columns):
-        c = meta_ref[1 + q]
-        sums[c] = sums[c] + terms[q]
+    for d in range(groups):
+        for q in range(2 * pieces):
+            c = place_ref[d * 2 * pieces + q]
+            sums[c] = sums[c] + terms[d * 2 * pieces + q]
     for c in range(columns):
         g, j = divmod(c, pieces)
         wide[pl.ds(g * per_group + j, rows, stride=pieces), :] = sums[c]
@@ -121,21 +125,6 @@
     lines = slots * CAP * pieces
     share = n_tp // own
 
-    down = jnp.swapaxes(adapter_down.reshape(own, rank, pieces, BLOCK), 1, 2)
-    weights = jnp.concatenate(
-        [
-            block_values.reshape(own, pieces * 2 * BLOCK, BLOCK),
-            down.reshape(own, pieces * rank, BLOCK),
-        ],
-        axis=1,
-    )
-    weights = jnp.repeat(weights, share, axis=0)
-    weights = lax.all_to_all(weights, "tp", 0, 0, tiled=True)
-    places = jnp.repeat(block_columns.reshape(own, pieces * 2), share, axis=0)
-    places = lax.all_to_all(places, "tp", 0, 0, tiled=True)
-    mine = (lax.axis_index("tp") // share).astype(i32)
-    meta = jnp.concatenate([mine[None], places.reshape(-1)])
-
     packed, target = pl.pallas_call(
         functools.partial(pack_kernel, n_tok, n_tp),
         out_shape=(
@@ -151,14 +140,39 @@
     )(token_adapter.reshape(1, tokens), adapter_slot.reshape(1, slots), attended)
     came = lax.all_to_all(packed, ("tp", "tok"), 0, 0, tiled=True)
 
+    here = lax.axis_index("tp")
+
+    packed, adapter_down, block_values, attended = lax.optimization_barrier(
+        (packed, adapter_down, block_values, attended)
+    )
+    spots = block_columns.reshape(own, pieces * 2, 1).astype(bf16)
+    down = jnp.swapaxes(adapter_down.reshape(own, rank, pieces, BLOCK), 1, 2)
+    held = jnp.concatenate(
+        [
+            block_values.reshape(own, pieces * 2 * BLOCK, BLOCK),
+            down.reshape(own, pieces * rank, BLOCK),
+            jnp.broadcast_to(spots, (own, pieces * 2, BLOCK)),
+        ],
+        axis=1,
+    )
+    weights = []
+    for d in range(n_tp):
+        part = lax.dynamic_index_in_dim(held, lax.rem(here + d, n_tp) // share, 0, False)
+        if d:
+            part = lax.ppermute(part, "tp", [(i, (i + d) % n_tp) for i in range(n_tp)])
+        weights.append(part)
+    at = jnp.stack([here, here // share]).astype(i32)
+
     base = jnp.dot(attended, output_weight, preferred_element_type=f32).astype(bf16)
+    places = jnp.concatenate([w[-2 * pieces :, 0] for w in weights]).astype(i32)
+    base, came, places, *weights = lax.optimization_barrier((base, came, places, *weights))
     base = lax.psum_scatter(base, "tp", scatter_dimension=1, tiled=True)
 
     rows = lines // pieces // n_tp
     deltas = pl.pallas_call(
         functools.partial(delta_kernel, n_tp),
         out_shape=jax.ShapeDtypeStruct((lines, BLOCK), bf16),
-        in_specs=[SMEM, VMEM, VMEM, VMEM],
+        in_specs=[SMEM, SMEM] + [VMEM] * (2 + n_tp),
         out_specs=VMEM,
         scratch_shapes=[
             pltpu.VMEM((lines, BLOCK), f32),
@@ -168,7 +182,7 @@
         compiler_params=PARAMS,
         cost_estimate=cost(6 * rows * columns * 2 * BLOCK, 8 * lines * BLOCK),
         name="slot_deltas",
-    )(meta, came, weights, adapter_up)
+    )(at, places, came, adapter_up, *weights)
     back = lax.all_to_all(deltas, ("tp", "tok"), 0, 0, tiled=True)
 
     return pl.pallas_call(

time: 210 us -> 156 us (0.74)
  waiting for transfers between devices: 84.5 us -> 40.8 us
  starting transfers between devices: 31.8 us -> 19.5 us
  blocking collectives: 48.4 us -> 52.9 us
    all_to_all x2 -> x0, waiting for transfers between devices: 44.4 us -> none  [the longest x1 44.4 us: on_device(): weights = lax.all_to_all(weights, 'tp', 0, 0, tiled=True)]
    all_to_all x1, waiting for transfers between devices: 40.1 us -> 0.01 us  [on_device(): came = lax.all_to_all(packed, ('tp', 'tok'), 0, 0, tiled=True)]
    ppermute x0 -> x3, waiting for transfers between devices: none -> 33.6 us  [on_device(): part = lax.ppermute(part, 'tp', [(i, (i + d) % n_tp) for i in range(n_tp)])]
    all_to_all x2 -> x0, starting transfers between devices: 9.21 us -> none  [the longest x1 4.84 us: on_device(): places = lax.all_to_all(places, 'tp', 0, 0, tiled=True)]
    reduce_scatter x1, waiting for transfers between devices: 0.01 us -> 7.13 us  [on_device(): base = lax.psum_scatter(base, 'tp', scatter_dimension=1, tiled=True)]
    all_to_all x1, starting transfers between devices: 22.6 us -> 15.7 us  [on_device(): came = lax.all_to_all(packed, ('tp', 'tok'), 0, 0, tiled=True)]
    all_to_all x1, blocking collectives: 48.4 us -> 52.9 us  [on_device(): back = lax.all_to_all(deltas, ('tp', 'tok'), 0, 0, tiled=True)]
    ppermute x0 -> x3, starting transfers between devices: none -> 3.75 us  [on_device(): part = lax.ppermute(part, 'tp', [(i, (i + d) % n_tp) for i in range(n_tp)])]
  transfers between devices with their start and end apart: 4 -> 5, of which waited for: 2 -> 4; matrix products, arithmetic and copies ran while one was open for 6% -> 9% of each run, Pallas kernels for 3% -> 3%
where the time goes in v2:
time: 156 us
  blocking collectives  52.9 us (34%)
  waiting for transfers between devices  40.8 us (26%)
  starting transfers between devices  19.5 us (12%)
  between operations  13.6 us (9%)
  Pallas kernels  11.1 us (7%)
  matrix products  9.41 us (6%)
  local copies, waits for them, and re-layouts  8.03 us (5%)
    all_to_all x1, blocking collectives, on_device(): back = lax.all_to_all(deltas, ('tp', 'tok'), 0, 0, tiled=True)  52.9 us
    ppermute x3, waiting for transfers between devices, on_device(): part = lax.ppermute(part, 'tp', [(i, (i + d) % n_tp) for i in range(n_tp)])  33.6 us
    all_to_all x1, starting transfers between devices, on_device(): came = lax.all_to_all(packed, ('tp', 'tok'), 0, 0, tiled=True)  15.7 us
    dot_general x1, matrix products, on_device(): jnp.dot(attended, output_weight, preferred_element_type=f32).astype(bf16)  9.41 us
    reduce_scatter x1, waiting for transfers between devices, on_device(): base = lax.psum_scatter(base, 'tp', scatter_dimension=1, tiled=True)  7.13 us
    pallas_call x1, Pallas kernels, on_device(): pl.pallas_call(functools.partial(delta_kernel, n_tp), out_shape=jax.Shape...  5.31 us
    unnamed x19, local copies, waits for them, and re-layouts  3.85 us
    ppermute x3, starting transfers between devices, on_device(): part = lax.ppermute(part, 'tp', [(i, (i + d) % n_tp) for i in range(n_tp)])  3.75 us
  transfers between devices with their start and end apart: 5, of which 4 were waited for; matrix products, arithmetic and copies ran while one was open for 9% of the time, Pallas kernels for 3%

profile of v2, /device:TPU:1, one launch (start us, length us, event | category | flops | bytes accessed | tf_op | source)
XLA Modules:
  0.0 155.6 jit_solution(15283359095441316282)
XLA Ops:
  6.5 1.2 copy-done.2
  7.8 0.7 copy-done.4
  8.4 0.7 copy-done.5
  9.1 2.8 %pack_rows.1 = (bf16[6144,128]{1,0:T(8,128)(2,1)}, s32[512,1]{1,0:T(8,128)S(1)}) custom-call(s32[1,512]{1,0:T(1,128)S(1)} %bitcast.31, s32[1,128]{1,0:T(1,128)S(1)} %bitcast.32, bf16[512,1024]{1,0:T(8,128)(2,1)S(1)} %copy-done.2), custom_call_target="tpu_custom_call" | custom-call | flops 805306368 | bytes 4718592 | tf_op jit(solution)/shard_map/pack_rows/pallas_call | solution.py:128
  11.9 15.7 %all-to-all-start = ((bf16[256,24,128]{2,1,0:T(8,128)(2,1)}), bf16[256,24,128]{2,1,0:T(8,128)(2,1)S(1)}, u32[]{:S(2)}, u32[]{:S(2)}) async-start(bf16[256,24,128]{2,1,0:T(8,128)(2,1)} %bitcast.4), calls=%async_computation | async-start | bytes 3145728 | tf_op jit(solution)/shard_map/all_to_all | solution.py:141
  27.6 0.0 reduce-scatter.2.cloned.1.call-start
  27.7 0.1 copy.12
  27.8 0.1 convert_element_type.19
  28.1 0.1 broadcast_in_dim.2
  28.2 0.1 pad_maximum_fusion
  28.2 0.0 copy-start.3
  28.3 1.4 dynamic-slice_bitcast_fusion.3
  29.6 2.6 %collective-permute-start.2 = (bf16[2576,128]{1,0:T(8,128)(2,1)}, bf16[2576,128]{1,0:T(8,128)(2,1)}, u32[]{:S(2)}, u32[]{:S(2)}) collective-permute-start(bf16[2576,128]{1,0:T(8,128)(2,1)} %get-tuple-element.30), channel_id=1, source_target_pairs={{0,3},{1,0},{2,1},{3,2},{4,7},{5,4},{6,5},{7,6},{8,11},{9,8},{10,9... | collective-permute-start | bytes 1978376 | tf_op jit(solution)/shard_map/ppermute | solution.py:162
  32.2 0.6 collective-permute-start.1
  32.8 0.6 collective-permute-start
  33.4 9.4 %convolution_convert_fusion = bf16[512,4096]{1,0:T(8,128)(2,1)} fusion(bf16[512,1024]{1,0:T(8,128)(2,1)S(1)} %copy-done.3, bf16[1024,4096]{1,0:T(8,128)(2,1)} %param.11), kind=kOutput, calls=%fused_computation | convolution fusion | flops 4297064448 | bytes 13631488 | tf_op jit(solution)/shard_map/dot_general | solution.py:166
  42.8 0.1 slice_reduce_fusion.3
  42.9 16.0 %collective-permute-done.2.refs_3_ = bf16[2576,128]{1,0:T(8,128)(2,1)} collective-permute-done((bf16[2576,128]{1,0:T(8,128)(2,1)}, bf16[2576,128]{1,0:T(8,128)(2,1)}, u32[]{:S(2)}, u32[]{:S(2)}) %collective-permute-start.2) | collective-permute-done | bytes 659488 | tf_op jit(solution)/shard_map/ppermute | solution.py:162
  59.0 0.8 slice_reduce_fusion
  59.7 1.4 collective-permute-done.1.refs_2_
  61.2 0.8 slice_reduce_fusion.1
  61.9 16.2 %collective-permute-done.refs_1_ = bf16[2576,128]{1,0:T(8,128)(2,1)} collective-permute-done((bf16[2576,128]{1,0:T(8,128)(2,1)}, bf16[2576,128]{1,0:T(8,128)(2,1)}, u32[]{:S(2)}, u32[]{:S(2)}) %collective-permute-start) | collective-permute-done | bytes 659488 | tf_op jit(solution)/shard_map/ppermute | solution.py:162
  78.1 0.8 slice_reduce_fusion.2
  78.9 0.1 maximum_convert_fusion.place_ref
  79.0 0.0 all-to-all-done
  79.0 0.0 reduce-scatter.2.cloned.1.call-update
  79.0 0.1 pad_add_fusion.at_ref
  79.1 5.3 %slot_deltas.1 = bf16[6144,128]{1,0:T(8,128)(2,1)S(1)} custom-call(s32[2]{0:T(128)S(1)} %pad_add_fusion.at_ref, s32[64]{0:T(128)S(1)} %maximum_convert_fusion.place_ref, bf16[6144,128]{1,0:T(8,128)(2,1)S(1)} %bitcast.28, bf16[2,64,4096]{2,1,0:T(8,128)(2,1)S(1)} %copy-done, bf16[2576,128]{1,0:T(8,128)(2,1)S(1)} %get-tuple-element.24.refs_0_, ...), custom_call_target="tpu_custom_call" | custom-call | flops 1207959552 | bytes 6291456 | tf_op jit(solution)/shard_map/slot_deltas/pallas_call | solution.py:172
  84.4 52.9 %all_to_all.23 = bf16[256,24,128]{2,1,0:T(8,128)(2,1)S(1)} all-to-all(bf16[256,24,128]{2,1,0:T(8,128)(2,1)S(1)} %bitcast.30), channel_id=1, replica_groups=mesh['tok'=64,'tp'=4] {'tp','tok'}, dimensions={0} | all-to-all | bytes 3145728 | tf_op jit(solution)/shard_map/all_to_all | solution.py:186
  137.3 7.1 %reduce-scatter.2.cloned.1.call-done.base_ref = bf16[512,1024]{1,0:T(8,128)(2,1)} async-done(((bf16[512,4096]{1,0:T(8,128)(2,1)}), bf16[512,1024]{1,0:T(8,128)(2,1)}) %reduce-scatter.2.cloned.1.call-update) | async-done | bytes 1048592 | tf_op jit(solution)/shard_map/reduce_scatter | solution.py:169
  144.5 1.2 copy-done.1
  145.7 3.0 %add_deltas.1 = bf16[512,1024]{1,0:T(8,128)(2,1)} custom-call(s32[512,1]{1,0:T(8,128)S(1)} %get-tuple-element.17.target_ref, bf16[6144,128]{1,0:T(8,128)(2,1)S(1)} %bitcast.29, bf16[512,1024]{1,0:T(8,128)(2,1)S(1)} %copy-done.1), custom_call_target="tpu_custom_call" | custom-call | flops 805306368 | bytes 4718592 | tf_op jit(solution)/shard_map/add_deltas/pallas_call | solution.py:188
  (17 shorter events, 0.1 us)
Async XLA Ops:
  6.5 1.2 copy-start.2
  7.8 0.7 copy-start.4
  8.4 0.7 copy-start.5
  9.1 18.6 %copy-start.8 = (s32[2,8,2]{1,2,0:T(2,128)S(1)}, s32[2,8,2]{1,2,0:T(2,128)}, u32[]{:S(2)}) copy-start(s32[2,8,2]{1,2,0:T(2,128)} %param.15) | copy-start | bytes 388
  9.1 18.8 %copy-start.7 = (bf16[2,64,1024]{2,1,0:T(8,128)(2,1)S(1)}, bf16[2,64,1024]{2,1,0:T(8,128)(2,1)}, u32[]{:S(2)}) copy-start(bf16[2,64,1024]{2,1,0:T(8,128)(2,1)} %param.12) | copy-start | bytes 786436
  11.9 16.3 %copy-start.6 = (bf16[2,8,2,128,128]{4,3,2,1,0:T(8,128)(2,1)S(1)}, bf16[2,8,2,128,128]{4,3,2,1,0:T(8,128)(2,1)}, u32[]{:S(2)}) copy-start(bf16[2,8,2,128,128]{4,3,2,1,0:T(8,128)(2,1)} %param.14) | copy-start | bytes 3145732
  11.9 67.1 %all-to-all-start = ((bf16[256,24,128]{2,1,0:T(8,128)(2,1)}), bf16[256,24,128]{2,1,0:T(8,128)(2,1)S(1)}, u32[]{:S(2)}, u32[]{:S(2)}) async-start(bf16[256,24,128]{2,1,0:T(8,128)(2,1)} %bitcast.4), calls=%async_computation | async-start | bytes 3145728 | tf_op jit(solution)/shard_map/all_to_all | solution.py:141
  27.6 116.9 %reduce-scatter.2.cloned.1.call-start = ((), (), s32[]{:S(2)}) async-start(), calls=%async_computation.3 | async-start | bytes 5242880 | tf_op jit(solution)/shard_map/reduce_scatter | solution.py:169
  28.2 5.1 %copy-start.3 = (bf16[512,1024]{1,0:T(8,128)(2,1)S(1)}, bf16[512,1024]{1,0:T(8,128)(2,1)}, u32[]{:S(2)}) copy-start(bf16[512,1024]{1,0:T(8,128)(2,1)} %x_ref.1) | copy-start | bytes 3145732
  29.6 29.3 %collective-permute-start.2 = (bf16[2576,128]{1,0:T(8,128)(2,1)}, bf16[2576,128]{1,0:T(8,128)(2,1)}, u32[]{:S(2)}, u32[]{:S(2)}) collective-permute-start(bf16[2576,128]{1,0:T(8,128)(2,1)} %get-tuple-element.30), channel_id=1, source_target_pairs={{0,3},{1,0},{2,1},{3,2},{4,7},{5,4},{6,5},{7,6},{8,11},{9,8},{10,9... | collective-permute-start | bytes 1978376 | tf_op jit(solution)/shard_map/ppermute | solution.py:162
  32.2 28.9 %collective-permute-start.1 = (bf16[2576,128]{1,0:T(8,128)(2,1)}, bf16[2576,128]{1,0:T(8,128)(2,1)}, u32[]{:S(2)}, u32[]{:S(2)}) collective-permute-start(bf16[2576,128]{1,0:T(8,128)(2,1)} %get-tuple-element.31), channel_id=1, source_target_pairs={{0,2},{1,3},{2,0},{3,1},{4,6},{5,7},{6,4},{7,5},{8,10},{9,11},{10,... | collective-permute-start | bytes 1978376 | tf_op jit(solution)/shard_map/ppermute | solution.py:162
  32.8 45.3 %collective-permute-start = (bf16[2576,128]{1,0:T(8,128)(2,1)}, bf16[2576,128]{1,0:T(8,128)(2,1)}, u32[]{:S(2)}, u32[]{:S(2)}) collective-permute-start(bf16[2576,128]{1,0:T(8,128)(2,1)} %get-tuple-element.32), channel_id=1, source_target_pairs={{0,1},{1,2},{2,3},{3,0},{4,5},{5,6},{6,7},{7,4},{8,9},{9,10},{10,1... | collective-permute-start | bytes 1978376 | tf_op jit(solution)/shard_map/ppermute | solution.py:162
  42.8 36.3 %copy-start = (bf16[2,64,4096]{2,1,0:T(8,128)(2,1)S(1)}, bf16[2,64,4096]{2,1,0:T(8,128)(2,1)}, u32[]{:S(2)}) copy-start(bf16[2,64,4096]{2,1,0:T(8,128)(2,1)} %up_ref.1) | copy-start | bytes 3145732
  144.5 1.2 copy-start.1
Sparse Core Ops, SparseCore 0:
  79.2 65.2 reduce-scatter.1

commit v3 on v2

v3 whole, which is shorter than its diff:
```python
import functools

import jax
import jax.numpy as jnp
from jax import lax
from jax.experimental import pallas as pl
from jax.experimental.pallas import tpu as pltpu
from jax.sharding import PartitionSpec as P

BLOCK = 128
CAP = 6
SCALE = 2.0
VMEM = pl.BlockSpec(memory_space=pltpu.VMEM)
SMEM = pl.BlockSpec(memory_space=pltpu.SMEM)
HBM = pl.BlockSpec(memory_space=pltpu.HBM)
PARAMS = pltpu.CompilerParams(vmem_limit_bytes=60 * 1024 * 1024)
f32, bf16, i32 = jnp.float32, jnp.bfloat16, jnp.int32


def iota(shape, dim):
    return lax.broadcasted_iota(i32, shape, dim)


def dot(a, b, dims=((1,), (0,))):
    return lax.dot_general(a, b, (dims, ((), ())), preferred_element_type=f32)


def pack_kernel(n_tok, n_tp, adapter_in, slot_in, x_in, out_ref, target_out, wide, adapter_ref, slot_ref, x_ref, target_ref, sems):
    copies = [
        pltpu.make_async_copy(src, dst, sems.at[i])
        for i, (src, dst) in enumerate(
            ((adapter_in, adapter_ref), (slot_in, slot_ref), (x_in, x_ref))
        )
    ]
    for copy in copies:
        copy.start()
    tokens, width = x_ref.shape
    slots = slot_ref.shape[1]
    pieces = width // BLOCK
    half = CAP // 2
    before = (iota((tokens, tokens), 0) < iota((tokens, tokens), 1)).astype(bf16)
    copies[0].wait()
    copies[1].wait()
    named = (iota((slots, tokens), 0) == adapter_ref[...]).astype(bf16)
    held = (iota((slots, slots), 0) == slot_ref[...]).astype(bf16)
    member = dot(held, named)
    count = dot(member.astype(bf16), before)
    rank = jnp.sum(member * count, axis=0, keepdims=True)
    slot = iota((slots, tokens), 0)
    base = (slot % n_tp) * (n_tok * half) + (slot // n_tp) * CAP
    start = jnp.sum(member * base.astype(f32), axis=0, keepdims=True)
    target = (start + rank).astype(i32)
    target_ref[...] = target
    send_target = pltpu.make_async_copy(target_ref, target_out, sems.at[3])
    send_target.start()
    rows = slots * CAP
    pick = (iota((rows, tokens), 0) == target).astype(bf16)
    copies[2].wait()
    for j in range(0, pieces, 2):
        both = dot(pick, x_ref[:, j * BLOCK : (j + 2) * BLOCK])
        wide[pl.ds(j, rows, stride=pieces), :] = both[:, :BLOCK]
        wide[pl.ds(j + 1, rows, stride=pieces), :] = both[:, BLOCK:]
    out_ref[...] = wide[...].astype(bf16)
    send_target.wait()


def delta_kernel(groups, at_ref, x_in, up_in, other_up_in, *refs):
    given = refs[: 2 * groups]
    out_ref, wide, terms, sums, x_ref, weights, ups, spots, places, sems = refs[2 * groups :]
    here, core, source = at_ref[0], at_ref[1], at_ref[2]
    per_group = x_ref.shape[0] // groups
    shares = [
        pl.ds(pl.multiple_of(lax.rem(here + groups - d, groups) * per_group, per_group), per_group)
        for d in range(groups)
    ]
    x_copies = [
        pltpu.make_async_copy(x_in.at[shares[d]], x_ref.at[pl.ds(d * per_group, per_group)], sems.at[2 * groups + 3 + d])
        for d in range(groups)
    ]
    copies = [
        pltpu.make_async_copy(given[i], weights.at[i], sems.at[i]) for i in range(2 * groups)
    ]
    own, rank, columns = up_in.shape
    up_copies = [
        pltpu.make_async_copy(up_in, ups.at[pl.ds(0, own)], sems.at[2 * groups]),
        pltpu.make_async_copy(other_up_in, ups.at[own], sems.at[2 * groups + 1]),
    ]
    for d in range(groups):
        x_copies[d].start()
        copies[d].start()
        copies[groups + d].start()
    for copy in up_copies:
        copy.start()
    columns = columns // BLOCK
    pieces = columns // groups
    some = pieces // 2
    rows = per_group // pieces
    shrunk = jnp.zeros((rows, rank), f32)
    down_at = pieces * BLOCK
    spots_at = down_at + some * rank

    def piece(d, j):
        return wide[pl.ds(d * per_group + j, rows, stride=pieces), :].astype(bf16)

    for d in range(groups):
        x_copies[d].wait()
        copies[d].wait()
        copies[groups + d].wait()
        own_rows = slice(d * per_group, (d + 1) * per_group)
        wide[own_rows, :] = x_ref[own_rows, :].astype(f32)
        spots[2 * pieces * d : 2 * pieces * (d + 1), :] = (
            weights[d, spots_at : spots_at + 2 * pieces, :].astype(f32).astype(i32)
        )
        for j in range(pieces):
            at = slice(j * BLOCK, (j + 1) * BLOCK)
            pair = jnp.concatenate([weights[d, at, :], weights[groups + d, at, :]], axis=1)
            both = dot(piece(d, j), pair)
            r = d * pieces + j
            terms[2 * r] = both[:, :BLOCK]
            terms[2 * r + 1] = both[:, BLOCK:]
        for j in range(some):
            at = slice(down_at + j * rank, down_at + (j + 1) * rank)
            x = jnp.concatenate([piece(d, core * some + j), piece(d, (1 - core) * some + j)], axis=1)
            down = jnp.concatenate([weights[d, at, :], weights[groups + d, at, :]], axis=1)
            shrunk = shrunk + dot(x, down, ((1,), (1,)))
    to_scalars = pltpu.make_async_copy(spots, places, sems.at[2 * groups + 2])
    to_scalars.start()
    small = (SCALE * shrunk).astype(bf16)
    for copy in up_copies:
        copy.wait()
    for c in range(0, columns, 2):
        both = dot(small, ups[source, :, c * BLOCK : (c + 2) * BLOCK])
        sums[c] = both[:, :BLOCK]
        sums[c + 1] = both[:, BLOCK:]
    to_scalars.wait()
    for r in range(columns):
        c = places[2 * r + core, 0]
        sums[c] = sums[c] + terms[2 * r]
        c = places[2 * r + 1 - core, 0]
        sums[c] = sums[c] + terms[2 * r + 1]
    out_copies = []
    for g in range(groups):
        for j in range(pieces):
            wide[pl.ds(g * per_group + j, rows, stride=pieces), :] = sums[g * pieces + j]
        own_rows = slice(g * per_group, (g + 1) * per_group)
        x_ref[own_rows, :] = wide[own_rows, :].astype(bf16)
        at = pl.ds(g * per_group, per_group)
        copy = pltpu.make_async_copy(x_ref.at[at], out_ref.at[at], sems.at[2 * groups + 3 + g])
        copy.start()
        out_copies.append(copy)
    for copy in out_copies:
        copy.wait()


def finish_kernel(target_in, back_in, base_in, out_ref, wide, target_ref, back_ref, base_ref, sems):
    get_target = pltpu.make_async_copy(target_in, target_ref, sems.at[0])
    get_base = pltpu.make_async_copy(base_in, base_ref, sems.at[1])
    get_back = pltpu.make_async_copy(back_in, back_ref, sems.at[2])
    get_target.start()
    get_back.start()
    get_base.start()
    tokens, width = base_ref.shape
    pieces = width // BLOCK
    rows = back_ref.shape[0] // pieces
    get_target.wait()
    eye = iota((tokens, tokens), 0) == iota((tokens, tokens), 1)
    target = jnp.sum(jnp.where(eye, target_ref[...], 0), axis=1, keepdims=True)
    pick = (iota((tokens, rows), 1) == target).astype(bf16)
    get_back.wait()
    wide[...] = back_ref[...].astype(f32)
    get_base.wait()
    for j in range(0, pieces, 2):
        part = jnp.concatenate(
            [wide[pl.ds(j + i, rows, stride=pieces), :].astype(bf16) for i in range(2)], axis=1
        )
        at = slice(j * BLOCK, (j + 2) * BLOCK)
        out_ref[:, at] = (dot(pick, part) + base_ref[:, at].astype(f32)).astype(bf16)


def cost(flops, moved):
    return pl.CostEstimate(flops=flops, bytes_accessed=moved, transcendentals=0)


def on_device(
    attended,
    token_adapter,
    adapter_slot,
    output_weight,
    adapter_down,
    adapter_up,
    block_values,
    block_columns,
):
    tokens, width = attended.shape
    slots = adapter_slot.shape[0]
    n_tok, n_tp = lax.axis_size("tok"), lax.axis_size("tp")
    own, rank = adapter_down.shape[:2]
    columns = adapter_up.shape[2]
    pieces = width // BLOCK
    lines = slots * CAP * pieces

    packed, target = pl.pallas_call(
        functools.partial(pack_kernel, n_tok, n_tp),
        out_shape=(
            jax.ShapeDtypeStruct((lines, BLOCK), bf16),
            jax.ShapeDtypeStruct((1, tokens), i32),
        ),
        in_specs=[HBM, HBM, HBM],
        out_specs=(VMEM, HBM),
        scratch_shapes=[
            pltpu.VMEM((lines, BLOCK), f32),
            pltpu.VMEM((1, tokens), i32),
            pltpu.VMEM((1, slots), i32),
            pltpu.VMEM((tokens, width), bf16),
            pltpu.VMEM((1, tokens), i32),
            pltpu.SemaphoreType.DMA((4,)),
        ],
        compiler_params=PARAMS,
        cost_estimate=cost(2 * lines // pieces * tokens * width, 6 * lines * BLOCK),
        name="pack_rows",
    )(token_adapter.reshape(1, tokens), adapter_slot.reshape(1, slots), attended)
    came = lax.all_to_all(packed, ("tp", "tok"), 0, 0, tiled=True)

    here, core = lax.axis_index("tp"), lax.axis_index("tok") % 2
    twins = [(i, i ^ 1) for i in range(n_tok)]

    packed, adapter_down, block_values, attended = lax.optimization_barrier(
        (packed, adapter_down, block_values, attended)
    )
    down = jnp.swapaxes(adapter_down.reshape(own, rank, pieces, BLOCK), 1, 2)
    spots = block_columns.reshape(own, pieces * 2, 1).astype(bf16)
    spots = jnp.broadcast_to(spots, (own, pieces * 2, BLOCK))
    halves = jnp.stack(
        [
            jnp.concatenate(
                [
                    block_values[:, :, h].reshape(own, pieces * BLOCK, BLOCK),
                    down[:, h * pieces // 2 : (h + 1) * pieces // 2].reshape(own, -1, BLOCK),
                    spots,
                ],
                axis=1,
            )
            for h in range(2)
        ]
    )
    kept = lax.dynamic_index_in_dim(halves, core, 0, False)
    sent = lax.dynamic_index_in_dim(halves, 1 - core, 0, False)
    got = lax.ppermute(sent, "tok", twins)
    near = []
    for d in range(n_tp):
        s = lax.rem(here + d, n_tp)
        own_part = lax.dynamic_index_in_dim(kept, s % own, 0, False)
        got_part = lax.dynamic_index_in_dim(got, s % own, 0, False)
        part = jnp.where(s // own == core, own_part, got_part)
        if d:
            part = lax.ppermute(part, "tp", [(i, (i + d) % n_tp) for i in range(n_tp)])
        near.append(part)
    base = jnp.dot(attended, output_weight, preferred_element_type=f32).astype(bf16)
    base, *near = lax.optimization_barrier((base, *near))
    far = [lax.ppermute(part, "tok", twins) for part in near]
    other_up = lax.ppermute(
        lax.dynamic_index_in_dim(adapter_up, here % own, 0, False), "tok", twins
    )
    at = jnp.stack([here, core, jnp.where(here // own == core, here % own, own)]).astype(i32)

    held = (base, came, other_up, *near, *far)
    base, came, other_up, *weights = lax.optimization_barrier(held)
    base = lax.psum_scatter(base, "tp", scatter_dimension=1, tiled=True)

    rows = lines // pieces // n_tp
    deltas = pl.pallas_call(
        functools.partial(delta_kernel, n_tp),
        out_shape=jax.ShapeDtypeStruct((lines, BLOCK), bf16),
        in_specs=[SMEM] + [HBM] * (3 + 2 * n_tp),
        out_specs=HBM,
        scratch_shapes=[
            pltpu.VMEM((lines, BLOCK), f32),
            pltpu.VMEM((2 * columns // BLOCK, rows, BLOCK), f32),
            pltpu.VMEM((columns // BLOCK, rows, BLOCK), f32),
            pltpu.VMEM((lines, BLOCK), bf16),
            pltpu.VMEM((2 * n_tp, *near[0].shape), bf16),
            pltpu.VMEM((own + 1, rank, columns), bf16),
            pltpu.VMEM((n_tp * 2 * pieces, BLOCK), i32),
            pltpu.SMEM((n_tp * 2 * pieces, BLOCK), i32),
            pltpu.SemaphoreType.DMA((3 * n_tp + 3,)),
        ],
        compiler_params=PARAMS,
        cost_estimate=cost(6 * rows * columns * 2 * BLOCK, 8 * lines * BLOCK),
        name="slot_deltas",
    )(at, came, adapter_up, other_up, *weights)
    back = lax.all_to_all(deltas, ("tp", "tok"), 0, 0, tiled=True)

    return pl.pallas_call(
        finish_kernel,
        out_shape=jax.ShapeDtypeStruct((tokens, width), bf16),
        in_specs=[HBM, HBM, HBM],
        out_specs=VMEM,
        scratch_shapes=[
            pltpu.VMEM((lines, BLOCK), f32),
            pltpu.VMEM((1, tokens), i32),
            pltpu.VMEM((lines, BLOCK), bf16),
            pltpu.VMEM((tokens, width), bf16),
            pltpu.SemaphoreType.DMA((3,)),
        ],
        compiler_params=PARAMS,
        cost_estimate=cost(2 * lines // pieces * tokens * width, 6 * lines * BLOCK),
        name="add_deltas",
    )(target, back, base)


def solution(mesh):
    placed = (
        P("tok", "tp"),
        P("tok", None),
        P(),
        P("tp", None),
        P("tok", None, "tp"),
        P("tok", None, None),
        P("tok", "tp", None, None, None),
        P("tok", "tp", None),
    )
    return jax.shard_map(
        on_device, mesh=mesh, in_specs=placed, out_specs=P("tok", "tp"), check_vma=False
    )
```

time: 156 us -> 145 us (0.929)
  waiting for transfers between devices: 40.8 us -> 19.8 us
  other arithmetic: 0.25 us -> 7.24 us
  Pallas kernels: 11.1 us -> 15 us
  starting transfers between devices: 19.5 us -> 22.7 us
  local copies, waits for them, and re-layouts: 8.03 us -> 5.1 us
    ppermute x3, waiting for transfers between devices: 33.6 us -> 14.3 us  [on_device(): part = lax.ppermute(part, 'tp', [(i, (i + d) % n_tp) for i in range(n_tp)])]
    ppermute x0 -> x6, starting transfers between devices: none -> 4.37 us  [the longest x4 2.22 us: on_device(): far = [lax.ppermute(part, 'tok', twins) for part in near]]
    select_n x0 -> x2, other arithmetic: none -> 4.27 us  [on_device(): part = jnp.where(s // own == core, own_part, got_part)]
    reduce_scatter x1, waiting for transfers between devices: 7.13 us -> 2.95 us  [on_device(): base = lax.psum_scatter(base, 'tp', scatter_dimension=1, tiled=True)]
    ppermute x0 -> x6, waiting for transfers between devices: none -> 2.6 us  [the longest x4 2.4 us: on_device(): far = [lax.ppermute(part, 'tok', twins) for part in near]]
    unnamed x19 -> x21, local copies, waits for them, and re-layouts: 3.85 us -> 1.27 us
    pallas_call x1, Pallas kernels: 5.31 us -> 7.45 us  [on_device(): pl.pallas_call(functools.partial(delta_kernel, n_tp), out_shape=jax.Shape...]
    another operation x1 -> x2, other arithmetic: 0.08 us -> 1.87 us  [the longest x1 1.2 us: on_device(): jnp.stack([jnp.concatenate([block_values[:, :, h].reshape(own, pieces * B...]
  transfers between devices with their start and end apart: 5 -> 11, of which waited for: 4 -> 9; matrix products, arithmetic and copies ran while one was open for 9% -> 14% of each run, Pallas kernels for 3% -> 5%
where the time goes in v3:
time: 145 us
  blocking collectives  52 us (36%)
  starting transfers between devices  22.7 us (16%)
  waiting for transfers between devices  19.8 us (14%)
  Pallas kernels  15 us (10%)
  between operations  13.6 us (9%)
  matrix products  9.38 us (6%)
  other arithmetic  7.24 us (5%)
  local copies, waits for them, and re-layouts  5.1 us (4%)
    all_to_all x1, blocking collectives, on_device(): back = lax.all_to_all(deltas, ('tp', 'tok'), 0, 0, tiled=True)  52 us
    all_to_all x1, starting transfers between devices, on_device(): came = lax.all_to_all(packed, ('tp', 'tok'), 0, 0, tiled=True)  15.7 us
    ppermute x3, waiting for transfers between devices, on_device(): part = lax.ppermute(part, 'tp', [(i, (i + d) % n_tp) for i in range(n_tp)])  14.3 us
    dot_general x1, matrix products, on_device(): jnp.dot(attended, output_weight, preferred_element_type=f32).astype(bf16)  9.38 us
    pallas_call x1, Pallas kernels, on_device(): pl.pallas_call(functools.partial(delta_kernel, n_tp), out_shape=jax.Shape...  7.45 us
    select_n x2, other arithmetic, on_device(): part = jnp.where(s // own == core, own_part, got_part)  4.27 us
    pallas_call x1, Pallas kernels, on_device(): pl.pallas_call(finish_kernel, out_shape=jax.ShapeDtypeStruct((tokens, wid...  3.87 us
    pallas_call x1, Pallas kernels, on_device(): pl.pallas_call(functools.partial(pack_kernel, n_tok, n_tp), out_shape=(ja...  3.7 us
  transfers between devices with their start and end apart: 11, of which 9 were waited for; matrix products, arithmetic and copies ran while one was open for 14% of the time, Pallas kernels for 5%

profile of v3, /device:TPU:1, one launch (start us, length us, event | category | flops | bytes accessed | tf_op | source)
XLA Modules:
  0.0 144.8 jit_solution(4773719111402668336)
XLA Ops:
  6.5 3.7 %pack_rows.1 = (bf16[6144,128]{1,0:T(8,128)(2,1)}, s32[1,512]{1,0:T(1,128)}) custom-call(s32[1,512]{1,0:T(1,128)} %bitcast.65, s32[1,128]{1,0:T(1,128)} %bitcast.66, bf16[512,1024]{1,0:T(8,128)(2,1)} %x_in.1), custom_call_target="tpu_custom_call" | custom-call | flops 805306368 | bytes 4718592 | tf_op jit(solution)/shard_map/pack_rows/pallas_call | solution.py:202
  10.3 15.7 %all-to-all-start = ((bf16[256,24,128]{2,1,0:T(8,128)(2,1)}), bf16[256,24,128]{2,1,0:T(8,128)(2,1)S(1)}, u32[]{:S(2)}, u32[]{:S(2)}) async-start(bf16[256,24,128]{2,1,0:T(8,128)(2,1)} %bitcast.60), calls=%async_computation | async-start | bytes 3145728 | tf_op jit(solution)/shard_map/all_to_all | solution.py:222
  26.0 0.1 copy.13
  26.4 0.7 copy.12
  27.2 0.9 fusion.16
  28.1 1.2 fusion.1
  29.3 1.1 fusion.3
  30.4 2.1 %collective-permute-start = (bf16[2,1296,128]{2,1,0:T(8,128)(2,1)}, bf16[2,1296,128]{2,1,0:T(8,128)(2,1)}, u32[]{:S(2)}, u32[]{:S(2)}) collective-permute-start(bf16[2,1296,128]{2,1,0:T(8,128)(2,1)} %fusion.3), channel_id=1, source_target_pairs={{0,4},{4,0},{8,12},{12,8},{16,20},{20,16},{24,28},{28,24},{32,36},... | collective-permute-start | bytes 1990664 | tf_op jit(solution)/shard_map/ppermute | solution.py:248
  32.6 1.9 %dynamic-slice_bitcast_fusion = bf16[64,4096]{1,0:T(8,128)(2,1)} fusion(bf16[2,64,4096]{2,1,0:T(8,128)(2,1)} %up_in.1, s32[]{:T(128)S(6)} %select_n.152), kind=kLoop, calls=%fused_computation.17 | loop fusion | bytes 1048580 | tf_op jit(solution)/shard_map/jit(dynamic_index_in_dim)/squeeze | solution.py:262
  34.5 0.2 collective-permute-done
  34.6 2.4 %fusion.6 = (bf16[1296,128]{1,0:T(8,128)(2,1)}, bf16[1296,128]{1,0:T(8,128)(2,1)S(1)}, bf16[1296,128]{1,0:T(8,128)(2,1)}) fusion(s32[]{:T(128)S(6)} %select_n.128, s32[]{:T(128)S(6)} %select_n.150, bf16[1,2,1296,128]{3,2,1,0:T(8,128)(2,1)S(1)} %get-tuple-element.55, bf16[1,2,1296,128]{3,2,1,0:T(8,128)(2,1)S(1)} %get-tuple-element.54, ...), kind=kLoop, calls=%fused_computation.20 | loop fusion | flops 995328 | bytes 3317791 | tf_op jit(solution)/shard_map/jit(_where)/select_n | solution.py:254
  37.1 0.8 collective-permute-start.3
  37.9 0.6 collective-permute-start.1
  38.5 1.9 %fusion.15 = bf16[1296,128]{1,0:T(8,128)(2,1)} fusion(s32[]{:T(128)S(6)} %select_n.128, s32[]{:T(128)S(6)} %select_n.144, bf16[1,2,1296,128]{3,2,1,0:T(8,128)(2,1)S(1)} %get-tuple-element.55, bf16[1,2,1296,128]{3,2,1,0:T(8,128)(2,1)S(1)} %get-tuple-element.54, bf16[2,1296,128]{2,1,0:T(8,128)(2,1)} %collective-permute-done, s32[]{:T(128)S(6)} %select_n.143, ...), kind=kLoop, calls=%fused_computation.29 | loop fusion | flops 331776 | bytes 1990669 | tf_op jit(solution)/shard_map/jit(_where)/select_n | solution.py:254
  40.4 1.1 collective-permute-start.2
  41.5 9.4 %convolution_convert_fusion = bf16[512,4096]{1,0:T(8,128)(2,1)} fusion(bf16[512,1024]{1,0:T(8,128)(2,1)S(1)} %copy-done.9, bf16[1024,4096]{1,0:T(8,128)(2,1)} %param.11), kind=kOutput, calls=%fused_computation | convolution fusion | flops 4297064448 | bytes 13631488 | tf_op jit(solution)/shard_map/dot_general | solution.py:258
  50.9 1.6 %collective-permute-done.3.refs_3_ = bf16[1296,128]{1,0:T(8,128)(2,1)} collective-permute-done((bf16[1296,128]{1,0:T(8,128)(2,1)}, bf16[1296,128]{1,0:T(8,128)(2,1)}, u32[]{:S(2)}, u32[]{:S(2)}) %collective-permute-start.3) | collective-permute-done | bytes 331808 | tf_op jit(solution)/shard_map/ppermute | solution.py:256
  52.5 1.6 %collective-permute-done.1.refs_1_ = bf16[1296,128]{1,0:T(8,128)(2,1)} collective-permute-done((bf16[1296,128]{1,0:T(8,128)(2,1)}, bf16[1296,128]{1,0:T(8,128)(2,1)}, u32[]{:S(2)}, u32[]{:S(2)}) %collective-permute-start.1) | collective-permute-done | bytes 331808 | tf_op jit(solution)/shard_map/ppermute | solution.py:256
  54.0 11.1 %collective-permute-done.2.refs_2_ = bf16[1296,128]{1,0:T(8,128)(2,1)S(1)} collective-permute-done((bf16[1296,128]{1,0:T(8,128)(2,1)}, bf16[1296,128]{1,0:T(8,128)(2,1)S(1)}, u32[]{:S(2)}, u32[]{:S(2)}) %collective-permute-start.2) | collective-permute-done | bytes 331808 | tf_op jit(solution)/shard_map/ppermute | solution.py:256
  65.2 1.6 %collective-permute-start.5 = (bf16[1296,128]{1,0:T(8,128)(2,1)S(1)}, bf16[1296,128]{1,0:T(8,128)(2,1)S(1)}, u32[]{:S(2)}, u32[]{:S(2)}) collective-permute-start(bf16[1296,128]{1,0:T(8,128)(2,1)S(1)} %get-tuple-element.38.refs_0_), channel_id=1, source_target_pairs={{0,4},{4,0},{8,12},{12,8},{16,20},{20,16},{24,28},{28,24},{32,36},... | collective-permute-start | bytes 995336 | tf_op jit(solution)/shard_map/ppermute | solution.py:260
  66.9 0.4 collective-permute-start.7
  67.4 0.6 collective-permute-done.5.refs_4_
  68.0 0.7 collective-permute-done.6.refs_5_
  68.7 0.7 collective-permute-done.7.refs_6_
  69.5 0.3 collective-permute-done.8.refs_7_
  69.8 0.3 copy-done.6
  70.2 0.8 copy-done
  71.0 0.7 pad_add_fusion.at_ref
  71.6 7.5 %slot_deltas.1 = bf16[6144,128]{1,0:T(8,128)(2,1)} custom-call(s32[3]{0:T(128)} %pad_add_fusion.at_ref, bf16[6144,128]{1,0:T(8,128)(2,1)} %bitcast.56, bf16[2,64,4096]{2,1,0:T(8,128)(2,1)} %up_in.1, bf16[64,4096]{1,0:T(8,128)(2,1)} %collective-permute-done.4.other_up_in, bf16[1296,128]{1,0:T(8,128)(2,1)} %copy-done.1, ...), custom_call_target="tpu_custom_call" | custom-call | flops 1207959552 | bytes 6291456 | tf_op jit(solution)/shard_map/slot_deltas/pallas_call | solution.py:271
  79.1 52.0 %all_to_all.23 = bf16[256,24,128]{2,1,0:T(8,128)(2,1)} all-to-all(bf16[256,24,128]{2,1,0:T(8,128)(2,1)} %bitcast.57), channel_id=1, replica_groups=mesh['tok'=64,'tp'=4] {'tp','tok'}, dimensions={0} | all-to-all | bytes 3145728 | tf_op jit(solution)/shard_map/all_to_all | solution.py:291
  131.1 2.9 %reduce-scatter.2.cloned.1.call-done.base_in = bf16[512,1024]{1,0:T(8,128)(2,1)} async-done(((bf16[512,4096]{1,0:T(8,128)(2,1)}), bf16[512,1024]{1,0:T(8,128)(2,1)}) %reduce-scatter.2.cloned.1.call-update) | async-done | bytes 1048592 | tf_op jit(solution)/shard_map/reduce_scatter | solution.py:268
  134.1 3.9 %add_deltas.1 = bf16[512,1024]{1,0:T(8,128)(2,1)} custom-call(s32[1,512]{1,0:T(1,128)} %get-tuple-element.26.target_in, bf16[6144,128]{1,0:T(8,128)(2,1)} %bitcast.55, bf16[512,1024]{1,0:T(8,128)(2,1)} %reduce-scatter.2.cloned.1.call-done.base_in), custom_call_target="tpu_custom_call" | custom-call | flops 805306368 | bytes 4718592 | tf_op jit(solution)/shard_map/add_deltas/pallas_call | solution.py:293
  (32 shorter events, 0.7 us)
Async XLA Ops:
  10.2 15.8 %copy-start.8 = (s32[2,8,2]{1,2,0:T(2,128)S(1)}, s32[2,8,2]{1,2,0:T(2,128)}, u32[]{:S(2)}) copy-start(s32[2,8,2]{1,2,0:T(2,128)} %param.15) | copy-start | bytes 388
  10.3 16.0 %copy-start.7 = (bf16[2,64,1024]{2,1,0:T(8,128)(2,1)S(1)}, bf16[2,64,1024]{2,1,0:T(8,128)(2,1)}, u32[]{:S(2)}) copy-start(bf16[2,64,1024]{2,1,0:T(8,128)(2,1)} %param.12) | copy-start | bytes 786436
  10.3 59.5 %all-to-all-start = ((bf16[256,24,128]{2,1,0:T(8,128)(2,1)}), bf16[256,24,128]{2,1,0:T(8,128)(2,1)S(1)}, u32[]{:S(2)}, u32[]{:S(2)}) async-start(bf16[256,24,128]{2,1,0:T(8,128)(2,1)} %bitcast.60), calls=%async_computation | async-start | bytes 3145728 | tf_op jit(solution)/shard_map/all_to_all | solution.py:222
  25.9 1.2 copy-start.2
  25.9 108.1 %reduce-scatter.2.cloned.1.call-start = ((), (), s32[]{:S(2)}) async-start(), calls=%async_computation.3 | async-start | bytes 5242880 | tf_op jit(solution)/shard_map/reduce_scatter | solution.py:268
  30.4 4.2 %collective-permute-start = (bf16[2,1296,128]{2,1,0:T(8,128)(2,1)}, bf16[2,1296,128]{2,1,0:T(8,128)(2,1)}, u32[]{:S(2)}, u32[]{:S(2)}) collective-permute-start(bf16[2,1296,128]{2,1,0:T(8,128)(2,1)} %fusion.3), channel_id=1, source_target_pairs={{0,4},{4,0},{8,12},{12,8},{16,20},{20,16},{24,28},{28,24},{32,36},... | collective-permute-start | bytes 1990664 | tf_op jit(solution)/shard_map/ppermute | solution.py:248
  34.4 32.9 %collective-permute-start.4 = (bf16[64,4096]{1,0:T(8,128)(2,1)}, bf16[64,4096]{1,0:T(8,128)(2,1)}, u32[]{:S(2)}, u32[]{:S(2)}) collective-permute-start(bf16[64,4096]{1,0:T(8,128)(2,1)} %dynamic-slice_bitcast_fusion), channel_id=1, source_target_pairs={{0,4},{4,0},{8,12},{12,8},{16,20},{20,16},{24,28},{28,24},{32,36},... | collective-permute-start | bytes 1572872 | tf_op jit(solution)/shard_map/ppermute | solution.py:261
  37.1 28.1 %copy-start.1 = (bf16[1296,128]{1,0:T(8,128)(2,1)}, bf16[1296,128]{1,0:T(8,128)(2,1)S(1)}, u32[]{:S(2)}) copy-start(bf16[1296,128]{1,0:T(8,128)(2,1)S(1)} %get-tuple-element.38.refs_0_) | copy-start | bytes 995332
  37.1 4.5 %copy-start.9 = (bf16[512,1024]{1,0:T(8,128)(2,1)S(1)}, bf16[512,1024]{1,0:T(8,128)(2,1)}, u32[]{:S(2)}) copy-start(bf16[512,1024]{1,0:T(8,128)(2,1)} %x_in.1) | copy-start | bytes 3145732
  37.1 15.4 %collective-permute-start.3 = (bf16[1296,128]{1,0:T(8,128)(2,1)}, bf16[1296,128]{1,0:T(8,128)(2,1)}, u32[]{:S(2)}, u32[]{:S(2)}) collective-permute-start(bf16[1296,128]{1,0:T(8,128)(2,1)} %get-tuple-element.47), channel_id=1, source_target_pairs={{0,3},{1,0},{2,1},{3,2},{4,7},{5,4},{6,5},{7,6},{8,11},{9,8},{10,9... | collective-permute-start | bytes 995336 | tf_op jit(solution)/shard_map/ppermute | solution.py:256
  37.9 16.1 %collective-permute-start.1 = (bf16[1296,128]{1,0:T(8,128)(2,1)}, bf16[1296,128]{1,0:T(8,128)(2,1)}, u32[]{:S(2)}, u32[]{:S(2)}) collective-permute-start(bf16[1296,128]{1,0:T(8,128)(2,1)} %get-tuple-element.49), channel_id=1, source_target_pairs={{0,1},{1,2},{2,3},{3,0},{4,5},{5,6},{6,7},{7,4},{8,9},{9,10},{10,1... | collective-permute-start | bytes 995336 | tf_op jit(solution)/shard_map/ppermute | solution.py:256
  40.4 24.8 %collective-permute-start.2 = (bf16[1296,128]{1,0:T(8,128)(2,1)}, bf16[1296,128]{1,0:T(8,128)(2,1)S(1)}, u32[]{:S(2)}, u32[]{:S(2)}) collective-permute-start(bf16[1296,128]{1,0:T(8,128)(2,1)} %fusion.15), channel_id=1, source_target_pairs={{0,2},{1,3},{2,0},{3,1},{4,6},{5,7},{6,4},{7,5},{8,10},{9,11},{10,... | collective-permute-start | bytes 995336 | tf_op jit(solution)/shard_map/ppermute | solution.py:256
  65.1 4.7 %copy-start.3 = (bf16[1296,128]{1,0:T(8,128)(2,1)}, bf16[1296,128]{1,0:T(8,128)(2,1)S(1)}, u32[]{:S(2)}) copy-start(bf16[1296,128]{1,0:T(8,128)(2,1)S(1)} %collective-permute-done.2.refs_2_) | copy-start | bytes 995332
  65.2 2.9 %collective-permute-start.5 = (bf16[1296,128]{1,0:T(8,128)(2,1)S(1)}, bf16[1296,128]{1,0:T(8,128)(2,1)S(1)}, u32[]{:S(2)}, u32[]{:S(2)}) collective-permute-start(bf16[1296,128]{1,0:T(8,128)(2,1)S(1)} %get-tuple-element.38.refs_0_), channel_id=1, source_target_pairs={{0,4},{4,0},{8,12},{12,8},{16,20},{20,16},{24,28},{28,24},{32,36},... | collective-permute-start | bytes 995336 | tf_op jit(solution)/shard_map/ppermute | solution.py:260
  66.8 1.9 %collective-permute-start.6 = (bf16[1296,128]{1,0:T(8,128)(2,1)}, bf16[1296,128]{1,0:T(8,128)(2,1)S(1)}, u32[]{:S(2)}, u32[]{:S(2)}) collective-permute-start(bf16[1296,128]{1,0:T(8,128)(2,1)} %collective-permute-done.1.refs_1_), channel_id=1, source_target_pairs={{0,4},{4,0},{8,12},{12,8},{16,20},{20,16},{24,28},{28,24},{32,36},... | collective-permute-start | bytes 995336 | tf_op jit(solution)/shard_map/ppermute | solution.py:260
  66.9 2.6 %collective-permute-start.7 = (bf16[1296,128]{1,0:T(8,128)(2,1)S(1)}, bf16[1296,128]{1,0:T(8,128)(2,1)S(1)}, u32[]{:S(2)}, u32[]{:S(2)}) collective-permute-start(bf16[1296,128]{1,0:T(8,128)(2,1)S(1)} %collective-permute-done.2.refs_2_), channel_id=1, source_target_pairs={{0,4},{4,0},{8,12},{12,8},{16,20},{20,16},{24,28},{28,24},{32,36},... | collective-permute-start | bytes 995336 | tf_op jit(solution)/shard_map/ppermute | solution.py:260
  67.3 2.5 %collective-permute-start.8 = (bf16[1296,128]{1,0:T(8,128)(2,1)}, bf16[1296,128]{1,0:T(8,128)(2,1)}, u32[]{:S(2)}, u32[]{:S(2)}) collective-permute-start(bf16[1296,128]{1,0:T(8,128)(2,1)} %collective-permute-done.3.refs_3_), channel_id=1, source_target_pairs={{0,4},{4,0},{8,12},{12,8},{16,20},{20,16},{24,28},{28,24},{32,36},... | collective-permute-start | bytes 995336 | tf_op jit(solution)/shard_map/ppermute | solution.py:260
  68.0 1.8 %copy-start.4 = (bf16[1296,128]{1,0:T(8,128)(2,1)}, bf16[1296,128]{1,0:T(8,128)(2,1)S(1)}, u32[]{:S(2)}) copy-start(bf16[1296,128]{1,0:T(8,128)(2,1)S(1)} %collective-permute-done.5.refs_4_) | copy-start | bytes 995332
  68.7 1.1 copy-start.5
  69.4 0.7 copy-start.6
  69.8 1.2 copy-start
Sparse Core Ops, SparseCore 0:
  69.9 64.0 reduce-scatter.1

commit v4 on v3

--- a/solution.py
+++ b/solution.py
@@ -5,11 +5,13 @@
 from jax import lax
 from jax.experimental import pallas as pl
 from jax.experimental.pallas import tpu as pltpu
+from jax.sharding import Mesh
 from jax.sharding import PartitionSpec as P
 
 BLOCK = 128
 CAP = 6
 SCALE = 2.0
+TOK = ("chip", "core")
 VMEM = pl.BlockSpec(memory_space=pltpu.VMEM)
 SMEM = pl.BlockSpec(memory_space=pltpu.SMEM)
 HBM = pl.BlockSpec(memory_space=pltpu.HBM)
@@ -152,13 +154,52 @@
         copy.wait()
 
 
-def finish_kernel(target_in, back_in, base_in, out_ref, wide, target_ref, back_ref, base_ref, sems):
+def base_kernel(chunk_ref, x_ref, w0_ref, w1_ref, *refs):
+    half = x_ref.shape[0] // 2
+    for i, w_ref in enumerate((w0_ref, w1_ref)):
+        total = dot(x_ref[i * half : (i + 1) * half, :], w_ref[...])
+        refs[i][...] = total.astype(bf16)
+
+
+def base_product(chunks, x, w, columns):
+    tokens, depth = x.shape
+    step = columns // 2
+    half = tokens // 2
+    part = pl.BlockSpec((half, step), lambda i, c: (0, i))
+    return pl.pallas_call(
+        base_kernel,
+        out_shape=[jax.ShapeDtypeStruct((half, columns), bf16)] * 2,
+        grid_spec=pltpu.PrefetchScalarGridSpec(
+            num_scalar_prefetch=1,
+            grid=(columns // step,),
+            in_specs=[
+                pl.BlockSpec((tokens, depth), lambda i, c: (0, 0)),
+                pl.BlockSpec((depth, step), lambda i, c: (0, c[0] * (columns // step) + i)),
+                pl.BlockSpec((depth, step), lambda i, c: (0, c[1] * (columns // step) + i)),
+            ],
+            out_specs=[part] * 2,
+        ),
+        compiler_params=PARAMS,
+        cost_estimate=cost(2 * tokens * depth * columns, 4 * depth * columns + 6 * tokens * depth),
+        name="base_product",
+    )(chunks, x, w, w)
+
+
+def finish_kernel(target_in, back_in, first_in, second_in, mine0_in, mine1_in, out_ref, wide, target_ref, back_ref, base_ref, mine_ref, sems):
     get_target = pltpu.make_async_copy(target_in, target_ref, sems.at[0])
-    get_base = pltpu.make_async_copy(base_in, base_ref, sems.at[1])
-    get_back = pltpu.make_async_copy(back_in, back_ref, sems.at[2])
+    get_back = pltpu.make_async_copy(back_in, back_ref, sems.at[1])
+    half = first_in.shape[0]
+    top, bottom = pl.ds(0, half), pl.ds(half, half)
+    others = [
+        pltpu.make_async_copy(first_in, base_ref.at[top], sems.at[2]),
+        pltpu.make_async_copy(second_in, base_ref.at[bottom], sems.at[3]),
+        pltpu.make_async_copy(mine0_in, mine_ref.at[top], sems.at[4]),
+        pltpu.make_async_copy(mine1_in, mine_ref.at[bottom], sems.at[5]),
+    ]
     get_target.start()
     get_back.start()
-    get_base.start()
+    for copy in others:
+        copy.start()
     tokens, width = base_ref.shape
     pieces = width // BLOCK
     rows = back_ref.shape[0] // pieces
@@ -168,13 +209,15 @@
     pick = (iota((tokens, rows), 1) == target).astype(bf16)
     get_back.wait()
     wide[...] = back_ref[...].astype(f32)
-    get_base.wait()
+    for copy in others:
+        copy.wait()
     for j in range(0, pieces, 2):
         part = jnp.concatenate(
             [wide[pl.ds(j + i, rows, stride=pieces), :].astype(bf16) for i in range(2)], axis=1
         )
         at = slice(j * BLOCK, (j + 2) * BLOCK)
-        out_ref[:, at] = (dot(pick, part) + base_ref[:, at].astype(f32)).astype(bf16)
+        base = mine_ref[:, at].astype(f32) + base_ref[:, at].astype(f32)
+        out_ref[:, at] = (dot(pick, part) + base).astype(bf16)
 
 
 def cost(flops, moved):
@@ -193,7 +236,7 @@
 ):
     tokens, width = attended.shape
     slots = adapter_slot.shape[0]
-    n_tok, n_tp = lax.axis_size("tok"), lax.axis_size("tp")
+    n_tok, n_tp = lax.axis_size(TOK), lax.axis_size("tp")
     own, rank = adapter_down.shape[:2]
     columns = adapter_up.shape[2]
     pieces = width // BLOCK
@@ -219,14 +262,27 @@
         cost_estimate=cost(2 * lines // pieces * tokens * width, 6 * lines * BLOCK),
         name="pack_rows",
     )(token_adapter.reshape(1, tokens), adapter_slot.reshape(1, slots), attended)
-    came = lax.all_to_all(packed, ("tp", "tok"), 0, 0, tiled=True)
-
-    here, core = lax.axis_index("tp"), lax.axis_index("tok") % 2
-    twins = [(i, i ^ 1) for i in range(n_tok)]
-
-    packed, adapter_down, block_values, attended = lax.optimization_barrier(
+    came = lax.all_to_all(packed, ("tp", "chip"), 0, 0, tiled=True)
+
+    here, core = lax.axis_index("tp"), lax.axis_index("core")
+    onward = [(i, (i + 1) % n_tp) for i in range(n_tp)]
+    backward = [(i, (i - 1) % n_tp) for i in range(n_tp)]
+    twins = [(0, 1), (1, 0)]
+
+    def ring_step(parts):
+        return [lax.ppermute(parts[0], "tp", onward), lax.ppermute(parts[1], "tp", backward)]
+
+    def product(offset, x):
+        chunks = lax.rem(jnp.stack([here + n_tp - offset, here + offset]), n_tp).astype(i32)
+        return base_product(chunks, x, output_weight, width)
+
+    def added(parts, more):
+        return [(a.astype(f32) + b.astype(f32)).astype(bf16) for a, b in zip(parts, more)]
+
+    packed, adapter_down, block_values, x = lax.optimization_barrier(
         (packed, adapter_down, block_values, attended)
     )
+
     down = jnp.swapaxes(adapter_down.reshape(own, rank, pieces, BLOCK), 1, 2)
     spots = block_columns.reshape(own, pieces * 2, 1).astype(bf16)
     spots = jnp.broadcast_to(spots, (own, pieces * 2, BLOCK))
@@ -245,27 +301,25 @@
     )
     kept = lax.dynamic_index_in_dim(halves, core, 0, False)
     sent = lax.dynamic_index_in_dim(halves, 1 - core, 0, False)
-    got = lax.ppermute(sent, "tok", twins)
+    got = lax.ppermute(sent, "core", twins)
+    other_up = lax.ppermute(
+        lax.dynamic_index_in_dim(adapter_up, here % own, 0, False), "core", twins
+    )
     near = []
     for d in range(n_tp):
         s = lax.rem(here + d, n_tp)
         own_part = lax.dynamic_index_in_dim(kept, s % own, 0, False)
         got_part = lax.dynamic_index_in_dim(got, s % own, 0, False)
-        part = jnp.where(s // own == core, own_part, got_part)
-        if d:
-            part = lax.ppermute(part, "tp", [(i, (i + d) % n_tp) for i in range(n_tp)])
-        near.append(part)
-    base = jnp.dot(attended, output_weight, preferred_element_type=f32).astype(bf16)
-    base, *near = lax.optimization_barrier((base, *near))
-    far = [lax.ppermute(part, "tok", twins) for part in near]
-    other_up = lax.ppermute(
-        lax.dynamic_index_in_dim(adapter_up, here % own, 0, False), "tok", twins
-    )
+        near.append(jnp.where(s // own == core, own_part, got_part))
+    *near, other_up, x = lax.optimization_barrier((*near, other_up, x))
+    for d in range(1, n_tp):
+        near[d] = lax.ppermute(near[d], "tp", [(i, (i + d) % n_tp) for i in range(n_tp)])
+    products = [y for offset in (1, 2, 3, 0) for y in product(offset, x)]
+    held = lax.optimization_barrier((*near, *products))
+    near, products = held[:n_tp], held[n_tp:]
+    far = [lax.ppermute(part, "core", twins) for part in near]
     at = jnp.stack([here, core, jnp.where(here // own == core, here % own, own)]).astype(i32)
-
-    held = (base, came, other_up, *near, *far)
-    base, came, other_up, *weights = lax.optimization_barrier(held)
-    base = lax.psum_scatter(base, "tp", scatter_dimension=1, tiled=True)
+    came, *weights = lax.optimization_barrier((came, *near, *far))
 
     rows = lines // pieces // n_tp
     deltas = pl.pallas_call(
@@ -288,37 +342,43 @@
         cost_estimate=cost(6 * rows * columns * 2 * BLOCK, 8 * lines * BLOCK),
         name="slot_deltas",
     )(at, came, adapter_up, other_up, *weights)
-    back = lax.all_to_all(deltas, ("tp", "tok"), 0, 0, tiled=True)
+    sums = ring_step(products[:2])
+    deltas, *sums = lax.optimization_barrier((deltas, *sums))
+    sums = ring_step(added(sums, products[2:4]))
+    sums = ring_step(added(sums, products[4:6]))
+    back = lax.all_to_all(deltas, ("tp", "chip"), 0, 0, tiled=True)
 
     return pl.pallas_call(
         finish_kernel,
         out_shape=jax.ShapeDtypeStruct((tokens, width), bf16),
-        in_specs=[HBM, HBM, HBM],
+        in_specs=[HBM] * 6,
         out_specs=VMEM,
         scratch_shapes=[
             pltpu.VMEM((lines, BLOCK), f32),
             pltpu.VMEM((1, tokens), i32),
             pltpu.VMEM((lines, BLOCK), bf16),
             pltpu.VMEM((tokens, width), bf16),
-            pltpu.SemaphoreType.DMA((3,)),
+            pltpu.VMEM((tokens, width), bf16),
+            pltpu.SemaphoreType.DMA((6,)),
         ],
         compiler_params=PARAMS,
         cost_estimate=cost(2 * lines // pieces * tokens * width, 6 * lines * BLOCK),
         name="add_deltas",
-    )(target, back, base)
+    )(target, back, *sums, *products[6:])
 
 
 def solution(mesh):
     placed = (
-        P("tok", "tp"),
-        P("tok", None),
+        P(TOK, "tp"),
+        P(TOK, None),
         P(),
         P("tp", None),
-        P("tok", None, "tp"),
-        P("tok", None, None),
-        P("tok", "tp", None, None, None),
-        P("tok", "tp", None),
-    )
+        P(TOK, None, "tp"),
+        P(TOK, None, None),
+        P(TOK, "tp", None, None, None),
+        P(TOK, "tp", None),
+    )
+    mesh = Mesh(mesh.devices.reshape(-1, 2, mesh.shape["tp"]), (*TOK, "tp"))
     return jax.shard_map(
-        on_device, mesh=mesh, in_specs=placed, out_specs=P("tok", "tp"), check_vma=False
-    )
+        on_device, mesh=mesh, in_specs=placed, out_specs=P(TOK, "tp"), check_vma=False
+    )

time: 145 us -> 136 us (0.938)
  blocking collectives: 52 us -> 0 us
  waiting for transfers between devices: 19.8 us -> 41.4 us
  starting transfers between devices: 22.7 us -> 44 us
  Pallas kernels: 15 us -> 34.4 us
  between operations: 13.6 us -> 0.45 us
  matrix products: 9.38 us -> 0 us
  local copies, waits for them, and re-layouts: 5.1 us -> 6.85 us
    all_to_all x1 -> x0, blocking collectives: 52 us -> none  [on_device(): back = lax.all_to_all(deltas, ('tp', 'tok'), 0, 0, tiled=True)]
    ppermute x8 -> x14, waiting for transfers between devices: 16.9 us -> 41.4 us  [the longest x3 33.7 us: ring_step(): lax.ppermute(parts[0], 'tp', onward)]
    pallas_call x0 -> x4, Pallas kernels: none -> 19 us  [base_product(): pl.pallas_call(base_kernel, out_shape=[jax.ShapeDtypeStruct((half, column...]
    all_to_all x1 -> x2, starting transfers between devices: 15.7 us -> 27.5 us  [the longest x1 16.5 us: on_device(): came = lax.all_to_all(packed, ('tp', 'chip'), 0, 0, tiled=True)]
    ppermute x8 -> x14, starting transfers between devices: 6.95 us -> 16.4 us  [the longest x3 7.11 us: ring_step(): lax.ppermute(parts[1], 'tp', backward)]
    dot_general x1 -> x0, matrix products: 9.38 us -> none  [on_device(): jnp.dot(attended, output_weight, preferred_element_type=f32).astype(bf16)]
    unnamed x21 -> x37, local copies, waits for them, and re-layouts: 1.27 us -> 5.29 us
    reduce_scatter x1 -> x0, waiting for transfers between devices: 2.95 us -> none  [on_device(): base = lax.psum_scatter(base, 'tp', scatter_dimension=1, tiled=True)]
  transfers between devices with their start and end apart: 11 -> 17, of which waited for: 9 -> 5; matrix products, arithmetic and copies ran while one was open for 14% -> 7% of each run, Pallas kernels for 5% -> 20%
where the time goes in v4:
time: 136 us; the launch traced here: 135 us
  starting transfers between devices  44 us (32%)
  waiting for transfers between devices  41.4 us (30%)
  Pallas kernels  34.4 us (25%)
  other arithmetic  8.17 us (6%)
  local copies, waits for them, and re-layouts  6.85 us (5%)
    ppermute x3, waiting for transfers between devices, ring_step(): lax.ppermute(parts[0], 'tp', onward)  33.7 us
    pallas_call x4, Pallas kernels, base_product(): pl.pallas_call(base_kernel, out_shape=[jax.ShapeDtypeStruct((half, column...  19 us
    all_to_all x1, starting transfers between devices, on_device(): came = lax.all_to_all(packed, ('tp', 'chip'), 0, 0, tiled=True)  16.5 us
    all_to_all x1, starting transfers between devices, on_device(): back = lax.all_to_all(deltas, ('tp', 'chip'), 0, 0, tiled=True)  11 us
    pallas_call x1, Pallas kernels, on_device(): pl.pallas_call(functools.partial(delta_kernel, n_tp), out_shape=jax.Shape...  7.49 us
    ppermute x3, starting transfers between devices, ring_step(): lax.ppermute(parts[1], 'tp', backward)  7.11 us
    ppermute x3, waiting for transfers between devices, on_device(): lax.ppermute(near[d], 'tp', [(i, (i + d) % n_tp) for i in range(n_tp)])  5.53 us
    unnamed x37, local copies, waits for them, and re-layouts  5.29 us
  transfers between devices with their start and end apart: 17, of which 5 were waited for; matrix products, arithmetic and copies ran while one was open for 7% of the time, Pallas kernels for 20%

profile of v4, /device:TPU:1, one launch (start us, length us, event | category | flops | bytes accessed | tf_op | source)
XLA Modules:
  0.0 135.2 jit_solution(12299107649117110745)
XLA Ops:
  0.0 3.7 %pack_rows.1 = (bf16[6144,128]{1,0:T(8,128)(2,1)}, s32[1,512]{1,0:T(1,128)}) custom-call(s32[1,512]{1,0:T(1,128)} %bitcast.67, s32[1,128]{1,0:T(1,128)} %bitcast.68, bf16[512,1024]{1,0:T(8,128)(2,1)} %x_ref.3), custom_call_target="tpu_custom_call" | custom-call | flops 805306368 | bytes 4718592 | tf_op jit(solution)/shard_map/pack_rows/pallas_call | solution.py:245
  3.7 16.5 %all-to-all-start = ((bf16[128,48,128]{2,1,0:T(8,128)(2,1)}), bf16[128,48,128]{2,1,0:T(8,128)(2,1)S(1)}, u32[]{:S(2)}, u32[]{:S(2)}) async-start(bf16[128,48,128]{2,1,0:T(8,128)(2,1)} %bitcast.62), calls=%async_computation | async-start | bytes 3145728 | tf_op jit(solution)/shard_map/all_to_all | solution.py:265
  21.7 1.1 fusion.3
  22.8 1.0 collective-permute-start
  23.7 1.1 dynamic-slice_bitcast_fusion
  26.2 1.9 %fusion.15 = bf16[1296,128]{1,0:T(8,128)(2,1)} fusion(s32[]{:T(128)S(6)} %select_n.123, s32[]{:T(128)S(6)} %select_n.139, bf16[1,2,1296,128]{3,2,1,0:T(8,128)(2,1)S(1)} %get-tuple-element.99, bf16[1,2,1296,128]{3,2,1,0:T(8,128)(2,1)S(1)} %get-tuple-element.98, bf16[2,1296,128]{2,1,0:T(8,128)(2,1)} %collective-permute-done, s32[]{:T(128)S(6)} %select_n.138, ...), kind=kLoop, calls=%fused_computation.32 | loop fusion | flops 331776 | bytes 1990669 | tf_op jit(solution)/shard_map/jit(_where)/select_n | solution.py:313
  28.1 2.4 %fusion.6 = (bf16[1296,128]{1,0:T(8,128)(2,1)}, bf16[1296,128]{1,0:T(8,128)(2,1)S(1)}, bf16[1296,128]{1,0:T(8,128)(2,1)}) fusion(s32[]{:T(128)S(6)} %select_n.123, s32[]{:T(128)S(6)} %select_n.145, bf16[1,2,1296,128]{3,2,1,0:T(8,128)(2,1)S(1)} %get-tuple-element.99, bf16[1,2,1296,128]{3,2,1,0:T(8,128)(2,1)S(1)} %get-tuple-element.98, ...), kind=kLoop, calls=%fused_computation.23 | loop fusion | flops 995328 | bytes 3317791 | tf_op jit(solution)/shard_map/jit(_where)/select_n | solution.py:313
  30.5 1.0 collective-permute-start.2
  31.5 2.8 %collective-permute-start.3 = (bf16[1296,128]{1,0:T(8,128)(2,1)}, bf16[1296,128]{1,0:T(8,128)(2,1)S(1)}, u32[]{:S(2)}, u32[]{:S(2)}) collective-permute-start(bf16[1296,128]{1,0:T(8,128)(2,1)} %fusion.15), channel_id=1, source_target_pairs={{0,2},{1,3},{2,0},{3,1},{4,6},{5,7},{6,4},{7,5},{8,10},{9,11},{10,... | collective-permute-start | bytes 995336 | tf_op jit(solution)/shard_map/ppermute | solution.py:316
  34.3 1.0 collective-permute-start.4
  35.3 4.8 %base_product.7 = (bf16[256,1024]{1,0:T(8,128)(2,1)}, bf16[256,1024]{1,0:T(8,128)(2,1)}) custom-call(s32[2]{0:T(128)} %get-tuple-element.100.chunk_ref, bf16[512,1024]{1,0:T(8,128)(2,1)} %x_ref.3, bf16[1024,4096]{1,0:T(8,128)(2,1)} %w1_ref.7, bf16[1024,4096]{1,0:T(8,128)(2,1)} %w1_ref.7), custom_call_target="tpu_custom_call" | custom-call | flops 1073741824 | bytes 7340032 | tf_op jit(solution)/shard_map/base_product/pallas_call | solution.py:169
  40.1 4.8 %base_product.6 = (bf16[256,1024]{1,0:T(8,128)(2,1)}, bf16[256,1024]{1,0:T(8,128)(2,1)}) custom-call(s32[2]{0:T(128)} %get-tuple-element.101.chunk_ref, bf16[512,1024]{1,0:T(8,128)(2,1)} %x_ref.3, bf16[1024,4096]{1,0:T(8,128)(2,1)} %w1_ref.7, bf16[1024,4096]{1,0:T(8,128)(2,1)} %w1_ref.7), custom_call_target="tpu_custom_call" | custom-call | flops 1073741824 | bytes 7340032 | tf_op jit(solution)/shard_map/base_product/pallas_call | solution.py:169
  44.8 4.7 %base_product.5 = (bf16[256,1024]{1,0:T(8,128)(2,1)}, bf16[256,1024]{1,0:T(8,128)(2,1)}) custom-call(s32[2]{0:T(128)} %get-tuple-element.102.chunk_ref, bf16[512,1024]{1,0:T(8,128)(2,1)} %x_ref.3, bf16[1024,4096]{1,0:T(8,128)(2,1)} %w1_ref.7, bf16[1024,4096]{1,0:T(8,128)(2,1)} %w1_ref.7), custom_call_target="tpu_custom_call" | custom-call | flops 1073741824 | bytes 7340032 | tf_op jit(solution)/shard_map/base_product/pallas_call | solution.py:169
  49.6 4.8 %base_product.4 = (bf16[256,1024]{1,0:T(8,128)(2,1)}, bf16[256,1024]{1,0:T(8,128)(2,1)}) custom-call(s32[2]{0:T(128)} %get-tuple-element.103.chunk_ref, bf16[512,1024]{1,0:T(8,128)(2,1)} %x_ref.3, bf16[1024,4096]{1,0:T(8,128)(2,1)} %w1_ref.7, bf16[1024,4096]{1,0:T(8,128)(2,1)} %w1_ref.7), custom_call_target="tpu_custom_call" | custom-call | flops 1073741824 | bytes 7340032 | tf_op jit(solution)/shard_map/base_product/pallas_call | solution.py:169
  54.3 5.5 %collective-permute-done.3.refs_2_ = bf16[1296,128]{1,0:T(8,128)(2,1)S(1)} collective-permute-done((bf16[1296,128]{1,0:T(8,128)(2,1)}, bf16[1296,128]{1,0:T(8,128)(2,1)S(1)}, u32[]{:S(2)}, u32[]{:S(2)}) %collective-permute-start.3) | collective-permute-done | bytes 331808 | tf_op jit(solution)/shard_map/ppermute | solution.py:316
  59.9 0.7 collective-permute-start.5
  60.8 2.5 %collective-permute-start.10 = (bf16[256,1024]{1,0:T(8,128)(2,1)}, bf16[256,1024]{1,0:T(8,128)(2,1)S(1)}, u32[]{:S(2)}, u32[]{:S(2)}) collective-permute-start(bf16[256,1024]{1,0:T(8,128)(2,1)} %get-tuple-element.81), channel_id=1, source_target_pairs={{0,3},{1,0},{2,1},{3,2},{4,7},{5,4},{6,5},{7,6},{8,11},{9,8},{10,9... | collective-permute-start | bytes 1572872 | tf_op jit(solution)/shard_map/ppermute | solution.py:273
  63.3 1.2 collective-permute-start.6
  64.5 0.7 copy-done.15
  66.4 1.0 collective-permute-done.8.refs_7_
  67.4 1.2 copy-done.1
  68.5 7.5 %slot_deltas.1 = bf16[6144,128]{1,0:T(8,128)(2,1)} custom-call(s32[3]{0:T(128)} %pad_add_fusion.at_ref, bf16[6144,128]{1,0:T(8,128)(2,1)} %bitcast.58, bf16[2,64,4096]{2,1,0:T(8,128)(2,1)} %up_in.1, bf16[64,4096]{1,0:T(8,128)(2,1)} %collective-permute-done.1.other_up_in, bf16[1296,128]{1,0:T(8,128)(2,1)} %copy-done.2, bf16[1296,128]{1,0:T(8,128)(2,1)} %copy-done.12, ...), custom_call_target="tpu_custom_call" | custom-call | flops 1207959552 | bytes 6291456 | tf_op jit(solution)/shard_map/slot_deltas/pallas_call | solution.py:325
  76.1 0.8 copy-done.8
  76.9 11.0 %all-to-all-start.1 = ((bf16[128,48,128]{2,1,0:T(8,128)(2,1)}), bf16[128,48,128]{2,1,0:T(8,128)(2,1)S(1)}, u32[]{:S(2)}, u32[]{:S(2)}) async-start(bf16[128,48,128]{2,1,0:T(8,128)(2,1)} %bitcast.59), calls=%async_computation.1 | async-start | bytes 3145728 | tf_op jit(solution)/shard_map/all_to_all | solution.py:349
  88.1 0.8 collective-permute-start.11
  89.3 2.4 %collective-permute-start.13 = (bf16[256,1024]{1,0:T(8,128)(2,1)S(1)}, bf16[256,1024]{1,0:T(8,128)(2,1)S(1)}, u32[]{:S(2)}, u32[]{:S(2)}) collective-permute-start(bf16[256,1024]{1,0:T(8,128)(2,1)S(1)} %add_convert_fusion.1), channel_id=1, source_target_pairs={{0,3},{1,0},{2,1},{3,2},{4,7},{5,4},{6,5},{7,6},{8,11},{9,8},{10,9... | collective-permute-start | bytes 1572872 | tf_op jit(solution)/shard_map/ppermute | solution.py:273
  91.7 19.3 %collective-permute-done.11 = bf16[256,1024]{1,0:T(8,128)(2,1)S(1)} collective-permute-done((bf16[256,1024]{1,0:T(8,128)(2,1)S(1)}, bf16[256,1024]{1,0:T(8,128)(2,1)S(1)}, u32[]{:S(2)}, u32[]{:S(2)}) %collective-permute-start.11) | collective-permute-done | bytes 524320 | tf_op jit(solution)/shard_map/ppermute | solution.py:273
  111.4 1.2 collective-permute-done.13
  112.8 2.2 %collective-permute-start.14 = (bf16[256,1024]{1,0:T(8,128)(2,1)S(1)}, bf16[256,1024]{1,0:T(8,128)(2,1)S(1)}, u32[]{:S(2)}, u32[]{:S(2)}) collective-permute-start(bf16[256,1024]{1,0:T(8,128)(2,1)S(1)} %add_convert_fusion), channel_id=1, source_target_pairs={{0,3},{1,0},{2,1},{3,2},{4,7},{5,4},{6,5},{7,6},{8,11},{9,8},{10,9... | collective-permute-start | bytes 1572872 | tf_op jit(solution)/shard_map/ppermute | solution.py:273
  115.0 14.4 %collective-permute-done.12.first_in = bf16[256,1024]{1,0:T(8,128)(2,1)S(1)} collective-permute-done((bf16[256,1024]{1,0:T(8,128)(2,1)S(1)}, bf16[256,1024]{1,0:T(8,128)(2,1)S(1)}, u32[]{:S(2)}, u32[]{:S(2)}) %collective-permute-start.12) | collective-permute-done | bytes 524320 | tf_op jit(solution)/shard_map/ppermute | solution.py:273
  129.4 0.8 copy-done.10
  130.9 4.2 %add_deltas.1 = bf16[512,1024]{1,0:T(8,128)(2,1)} custom-call(s32[1,512]{1,0:T(1,128)} %get-tuple-element.48.target_in, bf16[6144,128]{1,0:T(8,128)(2,1)} %bitcast.57, bf16[256,1024]{1,0:T(8,128)(2,1)} %copy-done.10, bf16[256,1024]{1,0:T(8,128)(2,1)} %copy-done.11, bf16[256,1024]{1,0:T(8,128)(2,1)} %get-tuple-element.89.mine0_in, ...), custom_call_target="tpu_custom_call" | custom-call | flops 805306368 | bytes 4718592 | tf_op jit(solution)/shard_map/add_deltas/pallas_call | solution.py:351
  (67 shorter events, 6.2 us)
Async XLA Ops:
  3.7 16.5 %copy-start.16 = (bf16[2,64,1024]{2,1,0:T(8,128)(2,1)S(1)}, bf16[2,64,1024]{2,1,0:T(8,128)(2,1)}, u32[]{:S(2)}) copy-start(bf16[2,64,1024]{2,1,0:T(8,128)(2,1)} %param.12) | copy-start | bytes 786436
  3.7 63.7 %all-to-all-start = ((bf16[128,48,128]{2,1,0:T(8,128)(2,1)}), bf16[128,48,128]{2,1,0:T(8,128)(2,1)S(1)}, u32[]{:S(2)}, u32[]{:S(2)}) async-start(bf16[128,48,128]{2,1,0:T(8,128)(2,1)} %bitcast.62), calls=%async_computation | async-start | bytes 3145728 | tf_op jit(solution)/shard_map/all_to_all | solution.py:265
  20.2 1.2 copy-start.3
  22.8 3.5 %collective-permute-start = (bf16[2,1296,128]{2,1,0:T(8,128)(2,1)}, bf16[2,1296,128]{2,1,0:T(8,128)(2,1)}, u32[]{:S(2)}, u32[]{:S(2)}) collective-permute-start(bf16[2,1296,128]{2,1,0:T(8,128)(2,1)} %fusion.3), channel_id=1, source_target_pairs={{0,4},{4,0},{1,5},{5,1},{2,6},{6,2},{3,7},{7,3},{8,12},{12,8},{9,1... | collective-permute-start | bytes 1990664 | tf_op jit(solution)/shard_map/ppermute | solution.py:304
  24.8 5.7 %collective-permute-start.1 = (bf16[64,4096]{1,0:T(8,128)(2,1)S(1)}, bf16[64,4096]{1,0:T(8,128)(2,1)}, u32[]{:S(2)}, u32[]{:S(2)}) collective-permute-start(bf16[64,4096]{1,0:T(8,128)(2,1)S(1)} %dynamic-slice_bitcast_fusion), channel_id=1, source_target_pairs={{0,4},{4,0},{1,5},{5,1},{2,6},{6,2},{3,7},{7,3},{8,12},{12,8},{9,1... | collective-permute-start | bytes 1572872 | tf_op jit(solution)/shard_map/ppermute | solution.py:305
  30.5 29.3 %copy-start.2 = (bf16[1296,128]{1,0:T(8,128)(2,1)}, bf16[1296,128]{1,0:T(8,128)(2,1)S(1)}, u32[]{:S(2)}) copy-start(bf16[1296,128]{1,0:T(8,128)(2,1)S(1)} %get-tuple-element.72.refs_0_) | copy-start | bytes 995332
  30.5 23.8 %collective-permute-start.2 = (bf16[1296,128]{1,0:T(8,128)(2,1)}, bf16[1296,128]{1,0:T(8,128)(2,1)S(1)}, u32[]{:S(2)}, u32[]{:S(2)}) collective-permute-start(bf16[1296,128]{1,0:T(8,128)(2,1)} %get-tuple-element.54), channel_id=1, source_target_pairs={{0,1},{1,2},{2,3},{3,0},{4,5},{5,6},{6,7},{7,4},{8,9},{9,10},{10,1... | collective-permute-start | bytes 995336 | tf_op jit(solution)/shard_map/ppermute | solution.py:316
  31.5 28.3 %collective-permute-start.3 = (bf16[1296,128]{1,0:T(8,128)(2,1)}, bf16[1296,128]{1,0:T(8,128)(2,1)S(1)}, u32[]{:S(2)}, u32[]{:S(2)}) collective-permute-start(bf16[1296,128]{1,0:T(8,128)(2,1)} %fusion.15), channel_id=1, source_target_pairs={{0,2},{1,3},{2,0},{3,1},{4,6},{5,7},{6,4},{7,5},{8,10},{9,11},{10,... | collective-permute-start | bytes 995336 | tf_op jit(solution)/shard_map/ppermute | solution.py:316
  34.3 25.5 %collective-permute-start.4 = (bf16[1296,128]{1,0:T(8,128)(2,1)}, bf16[1296,128]{1,0:T(8,128)(2,1)S(1)}, u32[]{:S(2)}, u32[]{:S(2)}) collective-permute-start(bf16[1296,128]{1,0:T(8,128)(2,1)} %get-tuple-element.56), channel_id=1, source_target_pairs={{0,3},{1,0},{2,1},{3,2},{4,7},{5,4},{6,5},{7,6},{8,11},{9,8},{10,9... | collective-permute-start | bytes 995336 | tf_op jit(solution)/shard_map/ppermute | solution.py:316
  54.3 13.0 %copy-start.12 = (bf16[1296,128]{1,0:T(8,128)(2,1)}, bf16[1296,128]{1,0:T(8,128)(2,1)S(1)}, u32[]{:S(2)}) copy-start(bf16[1296,128]{1,0:T(8,128)(2,1)S(1)} %collective-permute-done.2.refs_1_) | copy-start | bytes 995332
  59.9 7.5 %copy-start.13 = (bf16[1296,128]{1,0:T(8,128)(2,1)}, bf16[1296,128]{1,0:T(8,128)(2,1)S(1)}, u32[]{:S(2)}) copy-start(bf16[1296,128]{1,0:T(8,128)(2,1)S(1)} %collective-permute-done.3.refs_2_) | copy-start | bytes 995332
  59.9 4.7 %collective-permute-start.5 = (bf16[1296,128]{1,0:T(8,128)(2,1)S(1)}, bf16[1296,128]{1,0:T(8,128)(2,1)S(1)}, u32[]{:S(2)}, u32[]{:S(2)}) collective-permute-start(bf16[1296,128]{1,0:T(8,128)(2,1)S(1)} %get-tuple-element.72.refs_0_), channel_id=1, source_target_pairs={{0,4},{4,0},{1,5},{5,1},{2,6},{6,2},{3,7},{7,3},{8,12},{12,8},{9,1... | collective-permute-start | bytes 995336 | tf_op jit(solution)/shard_map/ppermute | solution.py:320
  60.7 15.4 %collective-permute-start.9 = (bf16[256,1024]{1,0:T(8,128)(2,1)}, bf16[256,1024]{1,0:T(8,128)(2,1)S(1)}, u32[]{:S(2)}, u32[]{:S(2)}) collective-permute-start(bf16[256,1024]{1,0:T(8,128)(2,1)} %get-tuple-element.80), channel_id=1, source_target_pairs={{0,1},{1,2},{2,3},{3,0},{4,5},{5,6},{6,7},{7,4},{8,9},{9,10},{10,1... | collective-permute-start | bytes 1572872 | tf_op jit(solution)/shard_map/ppermute | solution.py:273
  60.8 15.2 %collective-permute-start.10 = (bf16[256,1024]{1,0:T(8,128)(2,1)}, bf16[256,1024]{1,0:T(8,128)(2,1)S(1)}, u32[]{:S(2)}, u32[]{:S(2)}) collective-permute-start(bf16[256,1024]{1,0:T(8,128)(2,1)} %get-tuple-element.81), channel_id=1, source_target_pairs={{0,3},{1,0},{2,1},{3,2},{4,7},{5,4},{6,5},{7,6},{8,11},{9,8},{10,9... | collective-permute-start | bytes 1572872 | tf_op jit(solution)/shard_map/ppermute | solution.py:273
  63.3 3.0 %collective-permute-start.6 = (bf16[1296,128]{1,0:T(8,128)(2,1)S(1)}, bf16[1296,128]{1,0:T(8,128)(2,1)}, u32[]{:S(2)}, u32[]{:S(2)}) collective-permute-start(bf16[1296,128]{1,0:T(8,128)(2,1)S(1)} %collective-permute-done.2.refs_1_), channel_id=1, source_target_pairs={{0,4},{4,0},{1,5},{5,1},{2,6},{6,2},{3,7},{7,3},{8,12},{12,8},{9,1... | collective-permute-start | bytes 995336 | tf_op jit(solution)/shard_map/ppermute | solution.py:320
  64.5 1.9 %collective-permute-start.7 = (bf16[1296,128]{1,0:T(8,128)(2,1)S(1)}, bf16[1296,128]{1,0:T(8,128)(2,1)}, u32[]{:S(2)}, u32[]{:S(2)}) collective-permute-start(bf16[1296,128]{1,0:T(8,128)(2,1)S(1)} %collective-permute-done.3.refs_2_), channel_id=1, source_target_pairs={{0,4},{4,0},{1,5},{5,1},{2,6},{6,2},{3,7},{7,3},{8,12},{12,8},{9,1... | collective-permute-start | bytes 995336 | tf_op jit(solution)/shard_map/ppermute | solution.py:320
  65.3 2.1 %collective-permute-start.8 = (bf16[1296,128]{1,0:T(8,128)(2,1)}, bf16[1296,128]{1,0:T(8,128)(2,1)}, u32[]{:S(2)}, u32[]{:S(2)}) collective-permute-start(bf16[1296,128]{1,0:T(8,128)(2,1)} %copy-done.14), channel_id=1, source_target_pairs={{0,4},{4,0},{1,5},{5,1},{2,6},{6,2},{3,7},{7,3},{8,12},{12,8},{9,1... | collective-permute-start | bytes 995336 | tf_op jit(solution)/shard_map/ppermute | solution.py:320
  67.4 1.2 copy-start.1
  76.1 0.8 copy-start.8
  76.9 11.0 %copy-start.7 = (bf16[256,1024]{1,0:T(8,128)(2,1)S(1)}, bf16[256,1024]{1,0:T(8,128)(2,1)}, u32[]{:S(2)}) copy-start(bf16[256,1024]{1,0:T(8,128)(2,1)} %get-tuple-element.84) | copy-start | bytes 1572868
  76.9 52.5 %all-to-all-start.1 = ((bf16[128,48,128]{2,1,0:T(8,128)(2,1)}), bf16[128,48,128]{2,1,0:T(8,128)(2,1)S(1)}, u32[]{:S(2)}, u32[]{:S(2)}) async-start(bf16[128,48,128]{2,1,0:T(8,128)(2,1)} %bitcast.59), calls=%async_computation.1 | async-start | bytes 3145728 | tf_op jit(solution)/shard_map/all_to_all | solution.py:349
  87.9 1.0 copy-start.6
  87.9 1.2 copy-start.9
  87.9 23.1 %copy-start.5 = (bf16[256,1024]{1,0:T(8,128)(2,1)S(1)}, bf16[256,1024]{1,0:T(8,128)(2,1)}, u32[]{:S(2)}) copy-start(bf16[256,1024]{1,0:T(8,128)(2,1)} %get-tuple-element.85) | copy-start | bytes 1572868
  88.1 24.5 %copy-start.4 = (bf16[256,1024]{1,0:T(8,128)(2,1)S(1)}, bf16[256,1024]{1,0:T(8,128)(2,1)}, u32[]{:S(2)}) copy-start(bf16[256,1024]{1,0:T(8,128)(2,1)} %get-tuple-element.88) | copy-start | bytes 1572868
  88.1 22.9 %collective-permute-start.11 = (bf16[256,1024]{1,0:T(8,128)(2,1)S(1)}, bf16[256,1024]{1,0:T(8,128)(2,1)S(1)}, u32[]{:S(2)}, u32[]{:S(2)}) collective-permute-start(bf16[256,1024]{1,0:T(8,128)(2,1)S(1)} %add_convert_fusion.3), channel_id=1, source_target_pairs={{0,1},{1,2},{2,3},{3,0},{4,5},{5,6},{6,7},{7,4},{8,9},{9,10},{10,1... | collective-permute-start | bytes 1572872 | tf_op jit(solution)/shard_map/ppermute | solution.py:273
  89.3 23.3 %collective-permute-start.13 = (bf16[256,1024]{1,0:T(8,128)(2,1)S(1)}, bf16[256,1024]{1,0:T(8,128)(2,1)S(1)}, u32[]{:S(2)}, u32[]{:S(2)}) collective-permute-start(bf16[256,1024]{1,0:T(8,128)(2,1)S(1)} %add_convert_fusion.1), channel_id=1, source_target_pairs={{0,3},{1,0},{2,1},{3,2},{4,7},{5,4},{6,5},{7,6},{8,11},{9,8},{10,9... | collective-permute-start | bytes 1572872 | tf_op jit(solution)/shard_map/ppermute | solution.py:273
  111.2 18.2 %collective-permute-start.12 = (bf16[256,1024]{1,0:T(8,128)(2,1)S(1)}, bf16[256,1024]{1,0:T(8,128)(2,1)S(1)}, u32[]{:S(2)}, u32[]{:S(2)}) collective-permute-start(bf16[256,1024]{1,0:T(8,128)(2,1)S(1)} %add_convert_fusion.2), channel_id=1, source_target_pairs={{0,1},{1,2},{2,3},{3,0},{4,5},{5,6},{6,7},{7,4},{8,9},{9,10},{10,1... | collective-permute-start | bytes 1572872 | tf_op jit(solution)/shard_map/ppermute | solution.py:273
  112.8 16.6 %collective-permute-start.14 = (bf16[256,1024]{1,0:T(8,128)(2,1)S(1)}, bf16[256,1024]{1,0:T(8,128)(2,1)S(1)}, u32[]{:S(2)}, u32[]{:S(2)}) collective-permute-start(bf16[256,1024]{1,0:T(8,128)(2,1)S(1)} %add_convert_fusion), channel_id=1, source_target_pairs={{0,3},{1,0},{2,1},{3,2},{4,7},{5,4},{6,5},{7,6},{8,11},{9,8},{10,9... | collective-permute-start | bytes 1572872 | tf_op jit(solution)/shard_map/ppermute | solution.py:273
  129.4 0.8 copy-start.10
  129.4 1.0 copy-start.11
  129.4 1.5 %copy-start = (bf16[128,48,128]{2,1,0:T(8,128)(2,1)}, bf16[128,48,128]{2,1,0:T(8,128)(2,1)S(1)}, u32[]{:S(2)}) copy-start(bf16[128,48,128]{2,1,0:T(8,128)(2,1)S(1)} %all-to-all-done.1) | copy-start | bytes 4718596
  (3 other events, 2.2 us)

commit v5 on v4

--- a/solution.py
+++ b/solution.py
@@ -27,7 +27,7 @@
     return lax.dot_general(a, b, (dims, ((), ())), preferred_element_type=f32)
 
 
-def pack_kernel(n_tok, n_tp, adapter_in, slot_in, x_in, out_ref, target_out, wide, adapter_ref, slot_ref, x_ref, target_ref, sems):
+def pack_kernel(n_tok, n_tp, adapter_in, slot_in, x_in, out_ref, target_out, wide, adapter_ref, slot_ref, x_ref, target_ref, packed_ref, sems):
     copies = [
         pltpu.make_async_copy(src, dst, sems.at[i])
         for i, (src, dst) in enumerate(
@@ -56,14 +56,22 @@
     send_target = pltpu.make_async_copy(target_ref, target_out, sems.at[3])
     send_target.start()
     rows = slots * CAP
-    pick = (iota((rows, tokens), 0) == target).astype(bf16)
+    some = rows // n_tp
     copies[2].wait()
-    for j in range(0, pieces, 2):
-        both = dot(pick, x_ref[:, j * BLOCK : (j + 2) * BLOCK])
-        wide[pl.ds(j, rows, stride=pieces), :] = both[:, :BLOCK]
-        wide[pl.ds(j + 1, rows, stride=pieces), :] = both[:, BLOCK:]
-    out_ref[...] = wide[...].astype(bf16)
-    send_target.wait()
+    sends = []
+    for g in range(n_tp):
+        pick = (iota((some, tokens), 0) + g * some == target).astype(bf16)
+        first = g * some * pieces
+        for j in range(0, pieces, 2):
+            both = dot(pick, x_ref[:, j * BLOCK : (j + 2) * BLOCK])
+            wide[pl.ds(first + j, some, stride=pieces), :] = both[:, :BLOCK]
+            wide[pl.ds(first + j + 1, some, stride=pieces), :] = both[:, BLOCK:]
+        at = pl.ds(first, some * pieces)
+        packed_ref[at, :] = wide[at, :].astype(bf16)
+        sends.append(pltpu.make_async_copy(packed_ref.at[at], out_ref.at[at], sems.at[4 + g]))
+        sends[-1].start()
+    for copy in (send_target, *sends):
+        copy.wait()
 
 
 def delta_kernel(groups, at_ref, x_in, up_in, other_up_in, *refs):
@@ -154,14 +162,14 @@
         copy.wait()
 
 
-def base_kernel(chunk_ref, x_ref, w0_ref, w1_ref, *refs):
-    half = x_ref.shape[0] // 2
-    for i, w_ref in enumerate((w0_ref, w1_ref)):
-        total = dot(x_ref[i * half : (i + 1) * half, :], w_ref[...])
-        refs[i][...] = total.astype(bf16)
-
-
-def base_product(chunks, x, w, columns):
+def base_kernel(chunk_ref, x_ref, w_ref, top_ref, bottom_ref):
+    half = top_ref.shape[0]
+    total = dot(x_ref[...], w_ref[...]).astype(bf16)
+    top_ref[...] = total[:half]
+    bottom_ref[...] = total[half:]
+
+
+def base_product(chunk, x, w, columns):
     tokens, depth = x.shape
     step = columns // 2
     half = tokens // 2
@@ -175,32 +183,32 @@
             in_specs=[
                 pl.BlockSpec((tokens, depth), lambda i, c: (0, 0)),
                 pl.BlockSpec((depth, step), lambda i, c: (0, c[0] * (columns // step) + i)),
-                pl.BlockSpec((depth, step), lambda i, c: (0, c[1] * (columns // step) + i)),
             ],
             out_specs=[part] * 2,
         ),
         compiler_params=PARAMS,
-        cost_estimate=cost(2 * tokens * depth * columns, 4 * depth * columns + 6 * tokens * depth),
+        cost_estimate=cost(2 * tokens * depth * columns, 2 * depth * columns + 4 * tokens * depth),
         name="base_product",
-    )(chunks, x, w, w)
-
-
-def finish_kernel(target_in, back_in, first_in, second_in, mine0_in, mine1_in, out_ref, wide, target_ref, back_ref, base_ref, mine_ref, sems):
+    )(chunk, x, w)
+
+
+def finish_kernel(target_in, back_in, *refs):
+    terms, (out_ref, wide, target_ref, back_ref, base_ref, sems) = refs[:6], refs[6:]
     get_target = pltpu.make_async_copy(target_in, target_ref, sems.at[0])
     get_back = pltpu.make_async_copy(back_in, back_ref, sems.at[1])
-    half = first_in.shape[0]
-    top, bottom = pl.ds(0, half), pl.ds(half, half)
+    half = terms[0].shape[0]
     others = [
-        pltpu.make_async_copy(first_in, base_ref.at[top], sems.at[2]),
-        pltpu.make_async_copy(second_in, base_ref.at[bottom], sems.at[3]),
-        pltpu.make_async_copy(mine0_in, mine_ref.at[top], sems.at[4]),
-        pltpu.make_async_copy(mine1_in, mine_ref.at[bottom], sems.at[5]),
+        pltpu.make_async_copy(
+            terms[2 * i + j], base_ref.at[i, pl.ds(j * half, half)], sems.at[2 + 2 * i + j]
+        )
+        for i in range(3)
+        for j in range(2)
     ]
     get_target.start()
     get_back.start()
     for copy in others:
         copy.start()
-    tokens, width = base_ref.shape
+    tokens, width = base_ref.shape[1:]
     pieces = width // BLOCK
     rows = back_ref.shape[0] // pieces
     get_target.wait()
@@ -216,7 +224,7 @@
             [wide[pl.ds(j + i, rows, stride=pieces), :].astype(bf16) for i in range(2)], axis=1
         )
         at = slice(j * BLOCK, (j + 2) * BLOCK)
-        base = mine_ref[:, at].astype(f32) + base_ref[:, at].astype(f32)
+        base = base_ref[0, :, at].astype(f32) + base_ref[1, :, at].astype(f32) + base_ref[2, :, at].astype(f32)
         out_ref[:, at] = (dot(pick, part) + base).astype(bf16)
 
 
@@ -249,14 +257,15 @@
             jax.ShapeDtypeStruct((1, tokens), i32),
         ),
         in_specs=[HBM, HBM, HBM],
-        out_specs=(VMEM, HBM),
+        out_specs=(HBM, HBM),
         scratch_shapes=[
             pltpu.VMEM((lines, BLOCK), f32),
             pltpu.VMEM((1, tokens), i32),
             pltpu.VMEM((1, slots), i32),
             pltpu.VMEM((tokens, width), bf16),
             pltpu.VMEM((1, tokens), i32),
-            pltpu.SemaphoreType.DMA((4,)),
+            pltpu.VMEM((lines, BLOCK), bf16),
+            pltpu.SemaphoreType.DMA((4 + n_tp,)),
         ],
         compiler_params=PARAMS,
         cost_estimate=cost(2 * lines // pieces * tokens * width, 6 * lines * BLOCK),
@@ -269,15 +278,12 @@
     backward = [(i, (i - 1) % n_tp) for i in range(n_tp)]
     twins = [(0, 1), (1, 0)]
 
-    def ring_step(parts):
-        return [lax.ppermute(parts[0], "tp", onward), lax.ppermute(parts[1], "tp", backward)]
-
     def product(offset, x):
-        chunks = lax.rem(jnp.stack([here + n_tp - offset, here + offset]), n_tp).astype(i32)
-        return base_product(chunks, x, output_weight, width)
-
-    def added(parts, more):
-        return [(a.astype(f32) + b.astype(f32)).astype(bf16) for a, b in zip(parts, more)]
+        chunk = lax.rem(here + offset, n_tp).astype(i32)[None]
+        return base_product(chunk, x, output_weight, width)
+
+    def added(a, b):
+        return (a.astype(f32) + b.astype(f32)).astype(bf16)
 
     packed, adapter_down, block_values, x = lax.optimization_barrier(
         (packed, adapter_down, block_values, attended)
@@ -314,7 +320,7 @@
     *near, other_up, x = lax.optimization_barrier((*near, other_up, x))
     for d in range(1, n_tp):
         near[d] = lax.ppermute(near[d], "tp", [(i, (i + d) % n_tp) for i in range(n_tp)])
-    products = [y for offset in (1, 2, 3, 0) for y in product(offset, x)]
+    products = [y for offset in (2, 1, 3, 0) for y in product(offset, x)]
     held = lax.optimization_barrier((*near, *products))
     near, products = held[:n_tp], held[n_tp:]
     far = [lax.ppermute(part, "core", twins) for part in near]
@@ -342,29 +348,34 @@
         cost_estimate=cost(6 * rows * columns * 2 * BLOCK, 8 * lines * BLOCK),
         name="slot_deltas",
     )(at, came, adapter_up, other_up, *weights)
-    sums = ring_step(products[:2])
-    deltas, *sums = lax.optimization_barrier((deltas, *sums))
-    sums = ring_step(added(sums, products[2:4]))
-    sums = ring_step(added(sums, products[4:6]))
+    far_top, far_bottom, next_top, next_bottom, last_top, last_bottom, *mine = products
+    via_last = lax.ppermute(far_top, "tp", onward)
+    via_next = lax.ppermute(far_bottom, "tp", backward)
+    deltas, via_last, via_next = lax.optimization_barrier((deltas, via_last, via_next))
+    sums = [
+        lax.ppermute(added(next_top, via_last), "tp", onward),
+        lax.ppermute(next_bottom, "tp", onward),
+        lax.ppermute(last_top, "tp", backward),
+        lax.ppermute(added(last_bottom, via_next), "tp", backward),
+    ]
     back = lax.all_to_all(deltas, ("tp", "chip"), 0, 0, tiled=True)
 
     return pl.pallas_call(
         finish_kernel,
         out_shape=jax.ShapeDtypeStruct((tokens, width), bf16),
-        in_specs=[HBM] * 6,
+        in_specs=[HBM] * 8,
         out_specs=VMEM,
         scratch_shapes=[
             pltpu.VMEM((lines, BLOCK), f32),
             pltpu.VMEM((1, tokens), i32),
             pltpu.VMEM((lines, BLOCK), bf16),
-            pltpu.VMEM((tokens, width), bf16),
-            pltpu.VMEM((tokens, width), bf16),
-            pltpu.SemaphoreType.DMA((6,)),
+            pltpu.VMEM((3, tokens, width), bf16),
+            pltpu.SemaphoreType.DMA((8,)),
         ],
         compiler_params=PARAMS,
         cost_estimate=cost(2 * lines // pieces * tokens * width, 6 * lines * BLOCK),
         name="add_deltas",
-    )(target, back, *sums, *products[6:])
+    )(target, back, *sums, *mine)
 
 
 def solution(mesh):

time: 136 us -> 136 us (level)
  waiting for transfers between devices: 41.4 us -> 45.9 us
  Pallas kernels: 34.4 us -> 30.4 us
  other arithmetic: 8.17 us -> 5.78 us
  local copies, waits for them, and re-layouts: 6.85 us -> 8.28 us
    pallas_call x4, Pallas kernels: 19 us -> 15 us  [base_product(): pl.pallas_call(base_kernel, out_shape=[jax.ShapeDtypeStruct((half, column...]
    ppermute x3, waiting for transfers between devices: 5.53 us -> 9.29 us  [on_device(): lax.ppermute(near[d], 'tp', [(i, (i + d) % n_tp) for i in range(n_tp)])]
  transfers between devices with their start and end apart: 17 -> 17, of which waited for: 5 -> 8; matrix products, arithmetic and copies ran while one was open for 7% -> 6% of each run, Pallas kernels for 20% -> 17%
where the time goes in v5:
time: 136 us; the launch traced here: 135 us
  waiting for transfers between devices  45.9 us (34%)
  starting transfers between devices  44.5 us (33%)
  Pallas kernels  30.4 us (22%)
  local copies, waits for them, and re-layouts  8.28 us (6%)
  other arithmetic  5.78 us (4%)
    ppermute x1, waiting for transfers between devices, on_device(): lax.ppermute(next_bottom, 'tp', onward)  17.8 us
    ppermute x1, waiting for transfers between devices, on_device(): lax.ppermute(added(next_top, via_last), 'tp', onward)  17.3 us
    all_to_all x1, starting transfers between devices, on_device(): came = lax.all_to_all(packed, ('tp', 'chip'), 0, 0, tiled=True)  16.5 us
    pallas_call x4, Pallas kernels, base_product(): pl.pallas_call(base_kernel, out_shape=[jax.ShapeDtypeStruct((half, column...  15 us
    all_to_all x1, starting transfers between devices, on_device(): back = lax.all_to_all(deltas, ('tp', 'chip'), 0, 0, tiled=True)  11.8 us
    ppermute x3, waiting for transfers between devices, on_device(): lax.ppermute(near[d], 'tp', [(i, (i + d) % n_tp) for i in range(n_tp)])  9.29 us
    pallas_call x1, Pallas kernels, on_device(): pl.pallas_call(functools.partial(delta_kernel, n_tp), out_shape=jax.Shape...  7.48 us
    unnamed x37, local copies, waits for them, and re-layouts  5.92 us
  transfers between devices with their start and end apart: 17, of which 8 were waited for; matrix products, arithmetic and copies ran while one was open for 6% of the time, Pallas kernels for 17%

profile of v5, /device:TPU:1, one launch (start us, length us, event | category | flops | bytes accessed | tf_op | source)
XLA Modules:
  0.0 135.3 jit_solution(6065519878864442162)
XLA Ops:
  0.0 3.3 %pack_rows.1 = (bf16[6144,128]{1,0:T(8,128)(2,1)}, s32[1,512]{1,0:T(1,128)}) custom-call(s32[1,512]{1,0:T(1,128)} %bitcast.67, s32[1,128]{1,0:T(1,128)} %bitcast.68, bf16[512,1024]{1,0:T(8,128)(2,1)} %x_ref.3), custom_call_target="tpu_custom_call" | custom-call | flops 805306368 | bytes 4718592 | tf_op jit(solution)/shard_map/pack_rows/pallas_call | solution.py:253
  3.3 16.5 %all-to-all-start = ((bf16[128,48,128]{2,1,0:T(8,128)(2,1)}), bf16[128,48,128]{2,1,0:T(8,128)(2,1)S(1)}, u32[]{:S(2)}, u32[]{:S(2)}) async-start(bf16[128,48,128]{2,1,0:T(8,128)(2,1)} %bitcast.62), calls=%async_computation | async-start | bytes 3145728 | tf_op jit(solution)/shard_map/all_to_all | solution.py:274
  21.3 1.1 fusion.3
  22.4 1.0 collective-permute-start
  23.3 1.9 %dynamic-slice_bitcast_fusion = bf16[64,4096]{1,0:T(8,128)(2,1)} fusion(bf16[2,64,4096]{2,1,0:T(8,128)(2,1)} %up_in.1, s32[]{:T(128)S(6)} %select_n.147), kind=kLoop, calls=%fused_computation.18 | loop fusion | bytes 1048580 | tf_op jit(solution)/shard_map/jit(dynamic_index_in_dim)/squeeze | solution.py:312
  25.4 1.1 fusion.15
  26.5 2.5 %fusion.6 = (bf16[1296,128]{1,0:T(8,128)(2,1)}, bf16[1296,128]{1,0:T(8,128)(2,1)S(1)}, bf16[1296,128]{1,0:T(8,128)(2,1)}) fusion(s32[]{:T(128)S(6)} %select_n.123, s32[]{:T(128)S(6)} %select_n.145, bf16[1,2,1296,128]{3,2,1,0:T(8,128)(2,1)S(1)} %get-tuple-element.99, bf16[1,2,1296,128]{3,2,1,0:T(8,128)(2,1)S(1)} %get-tuple-element.98, ...), kind=kLoop, calls=%fused_computation.21 | loop fusion | flops 995328 | bytes 3317791 | tf_op jit(solution)/shard_map/jit(_where)/select_n | solution.py:319
  29.0 1.0 collective-permute-start.2
  30.0 2.8 %collective-permute-start.3 = (bf16[1296,128]{1,0:T(8,128)(2,1)S(1)}, bf16[1296,128]{1,0:T(8,128)(2,1)}, u32[]{:S(2)}, u32[]{:S(2)}) collective-permute-start(bf16[1296,128]{1,0:T(8,128)(2,1)S(1)} %fusion.15), channel_id=1, source_target_pairs={{0,2},{1,3},{2,0},{3,1},{4,6},{5,7},{6,4},{7,5},{8,10},{9,11},{10,... | collective-permute-start | bytes 995336 | tf_op jit(solution)/shard_map/ppermute | solution.py:322
  32.8 1.0 collective-permute-start.4
  33.8 3.8 %base_product.7 = (bf16[256,1024]{1,0:T(8,128)(2,1)}, bf16[256,1024]{1,0:T(8,128)(2,1)}) custom-call(s32[1]{0:T(128)} %bitcast.27.chunk_ref, bf16[512,1024]{1,0:T(8,128)(2,1)} %x_ref.3, bf16[1024,4096]{1,0:T(8,128)(2,1)} %w_ref.7), custom_call_target="tpu_custom_call" | custom-call | flops 1073741824 | bytes 4194304 | tf_op jit(solution)/shard_map/base_product/pallas_call | solution.py:177
  37.5 3.8 %base_product.6 = (bf16[256,1024]{1,0:T(8,128)(2,1)}, bf16[256,1024]{1,0:T(8,128)(2,1)}) custom-call(s32[1]{0:T(128)} %bitcast.26.chunk_ref, bf16[512,1024]{1,0:T(8,128)(2,1)} %x_ref.3, bf16[1024,4096]{1,0:T(8,128)(2,1)} %w_ref.7), custom_call_target="tpu_custom_call" | custom-call | flops 1073741824 | bytes 4194304 | tf_op jit(solution)/shard_map/base_product/pallas_call | solution.py:177
  41.3 3.8 %base_product.5 = (bf16[256,1024]{1,0:T(8,128)(2,1)}, bf16[256,1024]{1,0:T(8,128)(2,1)}) custom-call(s32[1]{0:T(128)} %bitcast.25.chunk_ref, bf16[512,1024]{1,0:T(8,128)(2,1)} %x_ref.3, bf16[1024,4096]{1,0:T(8,128)(2,1)} %w_ref.7), custom_call_target="tpu_custom_call" | custom-call | flops 1073741824 | bytes 4194304 | tf_op jit(solution)/shard_map/base_product/pallas_call | solution.py:177
  45.0 3.7 %base_product.4 = (bf16[256,1024]{1,0:T(8,128)(2,1)}, bf16[256,1024]{1,0:T(8,128)(2,1)}) custom-call(s32[1]{0:T(128)} %bitcast.24.chunk_ref, bf16[512,1024]{1,0:T(8,128)(2,1)} %x_ref.3, bf16[1024,4096]{1,0:T(8,128)(2,1)} %w_ref.7), custom_call_target="tpu_custom_call" | custom-call | flops 1073741824 | bytes 4194304 | tf_op jit(solution)/shard_map/base_product/pallas_call | solution.py:177
  48.8 9.3 %collective-permute-done.3.refs_2_ = bf16[1296,128]{1,0:T(8,128)(2,1)} collective-permute-done((bf16[1296,128]{1,0:T(8,128)(2,1)S(1)}, bf16[1296,128]{1,0:T(8,128)(2,1)}, u32[]{:S(2)}, u32[]{:S(2)}) %collective-permute-start.3) | collective-permute-done | bytes 331808 | tf_op jit(solution)/shard_map/ppermute | solution.py:322
  58.1 1.2 collective-permute-start.5
  59.5 2.4 %collective-permute-start.10 = (bf16[256,1024]{1,0:T(8,128)(2,1)}, bf16[256,1024]{1,0:T(8,128)(2,1)S(1)}, u32[]{:S(2)}, u32[]{:S(2)}) collective-permute-start(bf16[256,1024]{1,0:T(8,128)(2,1)} %get-tuple-element.81), channel_id=1, source_target_pairs={{0,3},{1,0},{2,1},{3,2},{4,7},{5,4},{6,5},{7,6},{8,11},{9,8},{10,9... | collective-permute-start | bytes 1572872 | tf_op jit(solution)/shard_map/ppermute | solution.py:353
  61.9 0.6 collective-permute-start.6
  62.6 0.7 copy-done.14
  63.8 0.6 pad_add_fusion.at_ref
  65.3 0.7 copy-done.15
  66.5 7.5 %slot_deltas.1 = bf16[6144,128]{1,0:T(8,128)(2,1)} custom-call(s32[3]{0:T(128)} %pad_add_fusion.at_ref, bf16[6144,128]{1,0:T(8,128)(2,1)} %bitcast.58, bf16[2,64,4096]{2,1,0:T(8,128)(2,1)} %up_in.1, bf16[64,4096]{1,0:T(8,128)(2,1)} %collective-permute-done.1.other_up_in, bf16[1296,128]{1,0:T(8,128)(2,1)} %copy-done.2, ...), custom_call_target="tpu_custom_call" | custom-call | flops 1207959552 | bytes 6291456 | tf_op jit(solution)/shard_map/slot_deltas/pallas_call | solution.py:331
  74.1 0.8 copy-done.8
  74.9 0.8 copy-done.6
  75.8 11.8 %all-to-all-start.1 = ((bf16[128,48,128]{2,1,0:T(8,128)(2,1)}), bf16[128,48,128]{2,1,0:T(8,128)(2,1)S(1)}, u32[]{:S(2)}, u32[]{:S(2)}) async-start(bf16[128,48,128]{2,1,0:T(8,128)(2,1)} %bitcast.59), calls=%async_computation.1 | async-start | bytes 3145728 | tf_op jit(solution)/shard_map/all_to_all | solution.py:361
  87.6 0.8 collective-permute-start.12
  88.3 2.0 %collective-permute-start.13 = (bf16[256,1024]{1,0:T(8,128)(2,1)}, bf16[256,1024]{1,0:T(8,128)(2,1)S(1)}, u32[]{:S(2)}, u32[]{:S(2)}) collective-permute-start(bf16[256,1024]{1,0:T(8,128)(2,1)} %get-tuple-element.86), channel_id=1, source_target_pairs={{0,3},{1,0},{2,1},{3,2},{4,7},{5,4},{6,5},{7,6},{8,11},{9,8},{10,9... | collective-permute-start | bytes 1572872 | tf_op jit(solution)/shard_map/ppermute | solution.py:358
  90.9 2.7 %collective-permute-start.14 = (bf16[256,1024]{1,0:T(8,128)(2,1)S(1)}, bf16[256,1024]{1,0:T(8,128)(2,1)S(1)}, u32[]{:S(2)}, u32[]{:S(2)}) collective-permute-start(bf16[256,1024]{1,0:T(8,128)(2,1)S(1)} %add_convert_fusion), channel_id=1, source_target_pairs={{0,3},{1,0},{2,1},{3,2},{4,7},{5,4},{6,5},{7,6},{8,11},{9,8},{10,9... | collective-permute-start | bytes 1572872 | tf_op jit(solution)/shard_map/ppermute | solution.py:359
  93.6 17.8 %collective-permute-done.12.refs_1_ = bf16[256,1024]{1,0:T(8,128)(2,1)S(1)} collective-permute-done((bf16[256,1024]{1,0:T(8,128)(2,1)}, bf16[256,1024]{1,0:T(8,128)(2,1)S(1)}, u32[]{:S(2)}, u32[]{:S(2)}) %collective-permute-start.12) | collective-permute-done | bytes 524320 | tf_op jit(solution)/shard_map/ppermute | solution.py:357
  111.7 17.3 %collective-permute-done.11.refs_0_ = bf16[256,1024]{1,0:T(8,128)(2,1)S(1)} collective-permute-done((bf16[256,1024]{1,0:T(8,128)(2,1)S(1)}, bf16[256,1024]{1,0:T(8,128)(2,1)S(1)}, u32[]{:S(2)}, u32[]{:S(2)}) %collective-permute-start.11) | collective-permute-done | bytes 524320 | tf_op jit(solution)/shard_map/ppermute | solution.py:356
  129.1 0.8 copy-done.12
  130.5 4.6 %add_deltas.1 = bf16[512,1024]{1,0:T(8,128)(2,1)} custom-call(s32[1,512]{1,0:T(1,128)} %get-tuple-element.48.target_in, bf16[6144,128]{1,0:T(8,128)(2,1)} %bitcast.57, bf16[256,1024]{1,0:T(8,128)(2,1)} %copy-done.12, bf16[256,1024]{1,0:T(8,128)(2,1)} %copy-done.10, bf16[256,1024]{1,0:T(8,128)(2,1)} %copy-done.11, bf16[256,1024]{1,0:T(8,128)(2,1)} %copy-done.13, ...), custom_call_target="tpu_custom_call" | custom-call | flops 805306368 | bytes 4718592 | tf_op jit(solution)/shard_map/add_deltas/pallas_call | solution.py:363
  (63 shorter events, 5.5 us)
Async XLA Ops:
  3.3 16.5 %copy-start.16 = (bf16[2,64,1024]{2,1,0:T(8,128)(2,1)S(1)}, bf16[2,64,1024]{2,1,0:T(8,128)(2,1)}, u32[]{:S(2)}) copy-start(bf16[2,64,1024]{2,1,0:T(8,128)(2,1)} %param.12) | copy-start | bytes 786436
  3.3 61.9 %all-to-all-start = ((bf16[128,48,128]{2,1,0:T(8,128)(2,1)}), bf16[128,48,128]{2,1,0:T(8,128)(2,1)S(1)}, u32[]{:S(2)}, u32[]{:S(2)}) async-start(bf16[128,48,128]{2,1,0:T(8,128)(2,1)} %bitcast.62), calls=%async_computation | async-start | bytes 3145728 | tf_op jit(solution)/shard_map/all_to_all | solution.py:274
  19.8 1.2 copy-start.3
  22.4 3.0 %collective-permute-start = (bf16[2,1296,128]{2,1,0:T(8,128)(2,1)}, bf16[2,1296,128]{2,1,0:T(8,128)(2,1)}, u32[]{:S(2)}, u32[]{:S(2)}) collective-permute-start(bf16[2,1296,128]{2,1,0:T(8,128)(2,1)} %fusion.3), channel_id=1, source_target_pairs={{0,4},{4,0},{1,5},{5,1},{2,6},{6,2},{3,7},{7,3},{8,12},{12,8},{9,1... | collective-permute-start | bytes 1990664 | tf_op jit(solution)/shard_map/ppermute | solution.py:310
  25.2 3.8 %collective-permute-start.1 = (bf16[64,4096]{1,0:T(8,128)(2,1)}, bf16[64,4096]{1,0:T(8,128)(2,1)}, u32[]{:S(2)}, u32[]{:S(2)}) collective-permute-start(bf16[64,4096]{1,0:T(8,128)(2,1)} %dynamic-slice_bitcast_fusion), channel_id=1, source_target_pairs={{0,4},{4,0},{1,5},{5,1},{2,6},{6,2},{3,7},{7,3},{8,12},{12,8},{9,1... | collective-permute-start | bytes 1572872 | tf_op jit(solution)/shard_map/ppermute | solution.py:311
  29.0 29.1 %copy-start.2 = (bf16[1296,128]{1,0:T(8,128)(2,1)}, bf16[1296,128]{1,0:T(8,128)(2,1)S(1)}, u32[]{:S(2)}) copy-start(bf16[1296,128]{1,0:T(8,128)(2,1)S(1)} %get-tuple-element.72.refs_0_) | copy-start | bytes 995332
  29.0 19.8 %collective-permute-start.2 = (bf16[1296,128]{1,0:T(8,128)(2,1)}, bf16[1296,128]{1,0:T(8,128)(2,1)}, u32[]{:S(2)}, u32[]{:S(2)}) collective-permute-start(bf16[1296,128]{1,0:T(8,128)(2,1)} %get-tuple-element.54), channel_id=1, source_target_pairs={{0,1},{1,2},{2,3},{3,0},{4,5},{5,6},{6,7},{7,4},{8,9},{9,10},{10,1... | collective-permute-start | bytes 995336 | tf_op jit(solution)/shard_map/ppermute | solution.py:322
  30.0 28.1 %collective-permute-start.3 = (bf16[1296,128]{1,0:T(8,128)(2,1)S(1)}, bf16[1296,128]{1,0:T(8,128)(2,1)}, u32[]{:S(2)}, u32[]{:S(2)}) collective-permute-start(bf16[1296,128]{1,0:T(8,128)(2,1)S(1)} %fusion.15), channel_id=1, source_target_pairs={{0,2},{1,3},{2,0},{3,1},{4,6},{5,7},{6,4},{7,5},{8,10},{9,11},{10,... | collective-permute-start | bytes 995336 | tf_op jit(solution)/shard_map/ppermute | solution.py:322
  32.8 25.3 %collective-permute-start.4 = (bf16[1296,128]{1,0:T(8,128)(2,1)}, bf16[1296,128]{1,0:T(8,128)(2,1)}, u32[]{:S(2)}, u32[]{:S(2)}) collective-permute-start(bf16[1296,128]{1,0:T(8,128)(2,1)} %get-tuple-element.56), channel_id=1, source_target_pairs={{0,3},{1,0},{2,1},{3,2},{4,7},{5,4},{6,5},{7,6},{8,11},{9,8},{10,9... | collective-permute-start | bytes 995336 | tf_op jit(solution)/shard_map/ppermute | solution.py:322
  58.1 4.5 %collective-permute-start.5 = (bf16[1296,128]{1,0:T(8,128)(2,1)S(1)}, bf16[1296,128]{1,0:T(8,128)(2,1)S(1)}, u32[]{:S(2)}, u32[]{:S(2)}) collective-permute-start(bf16[1296,128]{1,0:T(8,128)(2,1)S(1)} %get-tuple-element.72.refs_0_), channel_id=1, source_target_pairs={{0,4},{4,0},{1,5},{5,1},{2,6},{6,2},{3,7},{7,3},{8,12},{12,8},{9,1... | collective-permute-start | bytes 995336 | tf_op jit(solution)/shard_map/ppermute | solution.py:326
  59.2 14.9 %collective-permute-start.9 = (bf16[256,1024]{1,0:T(8,128)(2,1)}, bf16[256,1024]{1,0:T(8,128)(2,1)S(1)}, u32[]{:S(2)}, u32[]{:S(2)}) collective-permute-start(bf16[256,1024]{1,0:T(8,128)(2,1)} %get-tuple-element.80), channel_id=1, source_target_pairs={{0,1},{1,2},{2,3},{3,0},{4,5},{5,6},{6,7},{7,4},{8,9},{9,10},{10,1... | collective-permute-start | bytes 1572872 | tf_op jit(solution)/shard_map/ppermute | solution.py:352
  59.5 14.6 %collective-permute-start.10 = (bf16[256,1024]{1,0:T(8,128)(2,1)}, bf16[256,1024]{1,0:T(8,128)(2,1)S(1)}, u32[]{:S(2)}, u32[]{:S(2)}) collective-permute-start(bf16[256,1024]{1,0:T(8,128)(2,1)} %get-tuple-element.81), channel_id=1, source_target_pairs={{0,3},{1,0},{2,1},{3,2},{4,7},{5,4},{6,5},{7,6},{8,11},{9,8},{10,9... | collective-permute-start | bytes 1572872 | tf_op jit(solution)/shard_map/ppermute | solution.py:353
  61.9 2.5 %collective-permute-start.6 = (bf16[1296,128]{1,0:T(8,128)(2,1)}, bf16[1296,128]{1,0:T(8,128)(2,1)}, u32[]{:S(2)}, u32[]{:S(2)}) collective-permute-start(bf16[1296,128]{1,0:T(8,128)(2,1)} %collective-permute-done.2.refs_1_), channel_id=1, source_target_pairs={{0,4},{4,0},{1,5},{5,1},{2,6},{6,2},{3,7},{7,3},{8,12},{12,8},{9,1... | collective-permute-start | bytes 995336 | tf_op jit(solution)/shard_map/ppermute | solution.py:326
  62.6 2.1 %collective-permute-start.7 = (bf16[1296,128]{1,0:T(8,128)(2,1)}, bf16[1296,128]{1,0:T(8,128)(2,1)}, u32[]{:S(2)}, u32[]{:S(2)}) collective-permute-start(bf16[1296,128]{1,0:T(8,128)(2,1)} %collective-permute-done.3.refs_2_), channel_id=1, source_target_pairs={{0,4},{4,0},{1,5},{5,1},{2,6},{6,2},{3,7},{7,3},{8,12},{12,8},{9,1... | collective-permute-start | bytes 995336 | tf_op jit(solution)/shard_map/ppermute | solution.py:326
  63.3 2.0 %collective-permute-start.8 = (bf16[1296,128]{1,0:T(8,128)(2,1)}, bf16[1296,128]{1,0:T(8,128)(2,1)S(1)}, u32[]{:S(2)}, u32[]{:S(2)}) collective-permute-start(bf16[1296,128]{1,0:T(8,128)(2,1)} %collective-permute-done.4.refs_3_), channel_id=1, source_target_pairs={{0,4},{4,0},{1,5},{5,1},{2,6},{6,2},{3,7},{7,3},{8,12},{12,8},{9,1... | collective-permute-start | bytes 995336 | tf_op jit(solution)/shard_map/ppermute | solution.py:326
  65.3 1.3 copy-start.1
  74.1 0.8 copy-start.8
  74.9 0.8 copy-start.6
  74.9 15.4 %copy-start.5 = (bf16[256,1024]{1,0:T(8,128)(2,1)S(1)}, bf16[256,1024]{1,0:T(8,128)(2,1)}, u32[]{:S(2)}) copy-start(bf16[256,1024]{1,0:T(8,128)(2,1)} %get-tuple-element.83) | copy-start | bytes 1572868
  74.9 15.4 %copy-start.9 = (bf16[256,1024]{1,0:T(8,128)(2,1)S(1)}, bf16[256,1024]{1,0:T(8,128)(2,1)}, u32[]{:S(2)}) copy-start(bf16[256,1024]{1,0:T(8,128)(2,1)} %copy-done.8) | copy-start | bytes 1572868
  75.8 53.3 %all-to-all-start.1 = ((bf16[128,48,128]{2,1,0:T(8,128)(2,1)}), bf16[128,48,128]{2,1,0:T(8,128)(2,1)S(1)}, u32[]{:S(2)}, u32[]{:S(2)}) async-start(bf16[128,48,128]{2,1,0:T(8,128)(2,1)} %bitcast.59), calls=%async_computation.1 | async-start | bytes 3145728 | tf_op jit(solution)/shard_map/all_to_all | solution.py:361
  87.6 3.1 %copy-start.4 = (bf16[256,1024]{1,0:T(8,128)(2,1)S(1)}, bf16[256,1024]{1,0:T(8,128)(2,1)}, u32[]{:S(2)}) copy-start(bf16[256,1024]{1,0:T(8,128)(2,1)} %get-tuple-element.87) | copy-start | bytes 1572868
  87.6 3.1 %copy-start.7 = (bf16[256,1024]{1,0:T(8,128)(2,1)S(1)}, bf16[256,1024]{1,0:T(8,128)(2,1)}, u32[]{:S(2)}) copy-start(bf16[256,1024]{1,0:T(8,128)(2,1)} %copy-done.6) | copy-start | bytes 1572868
  87.6 23.8 %collective-permute-start.12 = (bf16[256,1024]{1,0:T(8,128)(2,1)}, bf16[256,1024]{1,0:T(8,128)(2,1)S(1)}, u32[]{:S(2)}, u32[]{:S(2)}) collective-permute-start(bf16[256,1024]{1,0:T(8,128)(2,1)} %get-tuple-element.85), channel_id=1, source_target_pairs={{0,1},{1,2},{2,3},{3,0},{4,5},{5,6},{6,7},{7,4},{8,9},{9,10},{10,1... | collective-permute-start | bytes 1572872 | tf_op jit(solution)/shard_map/ppermute | solution.py:357
  88.3 23.4 %collective-permute-start.13 = (bf16[256,1024]{1,0:T(8,128)(2,1)}, bf16[256,1024]{1,0:T(8,128)(2,1)S(1)}, u32[]{:S(2)}, u32[]{:S(2)}) collective-permute-start(bf16[256,1024]{1,0:T(8,128)(2,1)} %get-tuple-element.86), channel_id=1, source_target_pairs={{0,3},{1,0},{2,1},{3,2},{4,7},{5,4},{6,5},{7,6},{8,11},{9,8},{10,9... | collective-permute-start | bytes 1572872 | tf_op jit(solution)/shard_map/ppermute | solution.py:358
  90.6 38.5 %collective-permute-start.11 = (bf16[256,1024]{1,0:T(8,128)(2,1)S(1)}, bf16[256,1024]{1,0:T(8,128)(2,1)S(1)}, u32[]{:S(2)}, u32[]{:S(2)}) collective-permute-start(bf16[256,1024]{1,0:T(8,128)(2,1)S(1)} %add_convert_fusion.1), channel_id=1, source_target_pairs={{0,1},{1,2},{2,3},{3,0},{4,5},{5,6},{6,7},{7,4},{8,9},{9,10},{10,1... | collective-permute-start | bytes 1572872 | tf_op jit(solution)/shard_map/ppermute | solution.py:356
  90.9 38.2 %collective-permute-start.14 = (bf16[256,1024]{1,0:T(8,128)(2,1)S(1)}, bf16[256,1024]{1,0:T(8,128)(2,1)S(1)}, u32[]{:S(2)}, u32[]{:S(2)}) collective-permute-start(bf16[256,1024]{1,0:T(8,128)(2,1)S(1)} %add_convert_fusion), channel_id=1, source_target_pairs={{0,3},{1,0},{2,1},{3,2},{4,7},{5,4},{6,5},{7,6},{8,11},{9,8},{10,9... | collective-permute-start | bytes 1572872 | tf_op jit(solution)/shard_map/ppermute | solution.py:359
  111.4 17.7 %copy-start.10 = (bf16[256,1024]{1,0:T(8,128)(2,1)}, bf16[256,1024]{1,0:T(8,128)(2,1)S(1)}, u32[]{:S(2)}) copy-start(bf16[256,1024]{1,0:T(8,128)(2,1)S(1)} %collective-permute-done.12.refs_1_) | copy-start | bytes 1572868
  111.7 17.3 %copy-start.11 = (bf16[256,1024]{1,0:T(8,128)(2,1)}, bf16[256,1024]{1,0:T(8,128)(2,1)S(1)}, u32[]{:S(2)}) copy-start(bf16[256,1024]{1,0:T(8,128)(2,1)S(1)} %collective-permute-done.13.refs_2_) | copy-start | bytes 1572868
  129.1 0.8 copy-start.12
  129.1 1.0 copy-start.13
  129.1 1.5 %copy-start = (bf16[128,48,128]{2,1,0:T(8,128)(2,1)}, bf16[128,48,128]{2,1,0:T(8,128)(2,1)S(1)}, u32[]{:S(2)}) copy-start(bf16[128,48,128]{2,1,0:T(8,128)(2,1)S(1)} %all-to-all-done.1) | copy-start | bytes 4718596
  (3 other events, 2.2 us)
